TPU v7x, 32 devices: a whole 2x2x4 slice. The times are simulated.
32 devices in a mesh: dom: 8 (over z, core), band: 4 (over y, x).
Axes of the slice: x: 2, y: 2, z: 4, core: 2. Of those that a mesh axis runs over, the one named last changes fastest.
Arguments:
- block: float32 [16384, 256], P('dom', 'band'), may hold values from -8 to 8
- locked: float32 [16384, 8192], P('dom', 'band'), may hold values from -1.1 to 1.1
Outputs:
- basis: float32 [16384, 256], P('dom', 'band')
- coefficients: float32 [8192, 256], P('band')
All inputs are finite; a program needn't handle non-finite values.
Results may differ from a plain program's by a relative error of at most 0.0003.
Values sent between devices are 32-bit elements; how exact they have to be, the bound alone decides.
No kernel may reach another device: no remote copies, remote signals or barrier semaphores. Data moves between devices by JAX's collectives and lax.ppermute only.
A program may use at most 64 MiB of HBM per device.

v0:
```python
import functools

import jax
import jax.numpy as jnp
from jax import lax
from jax.experimental import pallas as pl
from jax.experimental.pallas import tpu as pltpu
from jax.sharding import PartitionSpec as P

CHUNKS = 2
TURNS = "AAABABABABABABABABABABBB"
f32 = jnp.float32


def swap(x, axis, k):
    n = lax.axis_size(axis)
    return lax.ppermute(x, axis, [(i, i ^ k) for i in range(n)])


def bits(n):
    return [1 << i for i in range(n.bit_length() - 1)]


VMEM = pl.BlockSpec(memory_space=pltpu.VMEM)
SMEM = pl.BlockSpec(memory_space=pltpu.SMEM)
HBM = pl.BlockSpec(memory_space=pl.ANY)
LIMIT = pltpu.CompilerParams(vmem_limit_bytes=8 << 20)
SLOTS = 4


def split(x):
    high = x.astype(jnp.bfloat16)
    return high, (x - high.astype(f32)).astype(jnp.bfloat16)


def split_kernel(x_ref, parts_ref, slots, sems):
    size = slots.shape[1]
    count = x_ref.shape[0] // size

    def copy(i):
        return pltpu.make_async_copy(
            x_ref.at[pl.ds(i * size, size)], slots.at[i % SLOTS], sems.at[i % SLOTS]
        )

    for i in range(min(SLOTS, count)):
        copy(i).start()
    for i in range(count):
        copy(i).wait()
        high, low = split(slots[i % SLOTS])
        parts_ref[0, pl.ds(i * size, size), :] = high
        parts_ref[1, pl.ds(i * size, size), :] = low
        if i + SLOTS < count:
            copy(i + SLOTS).start()


def split_array(x):
    size = 128
    return pl.pallas_call(
        split_kernel,
        out_shape=jax.ShapeDtypeStruct((2, *x.shape), jnp.bfloat16),
        in_specs=[HBM],
        out_specs=VMEM,
        scratch_shapes=[
            pltpu.VMEM((SLOTS, size, x.shape[1]), f32),
            pltpu.SemaphoreType.DMA((SLOTS,)),
        ],
        compiler_params=LIMIT,
        name="split_array",
    )(x)


def product_kernel(place_ref, *refs, spans, dim, block, by_rows):
    count = len(spans)
    ins, parts, outs = refs[:count], refs[count], refs[count + 1 : -2]
    rows_ref, both_ref = refs[-2:]
    mask = place_ref[0]
    n = rows_ref.shape[0]
    w = 0
    for ref, span in zip(ins, spans):
        for i in range(*span, block):
            at = pl.multiple_of((w ^ mask) * block, block)
            rows_ref[pl.ds(at, block), :] = ref[i : i + block, :]
            w += 1
    both_ref[:n, :], both_ref[n:, :] = split(rows_ref[...])
    dims = (((1,), (dim,)), ((), ()))

    def slab(ref, start, size):
        if dim == 0:
            return parts[ref, :, pl.ds(start, size)]
        return parts[ref, pl.ds(start, size), :]

    def multiply(start, size):
        part = lax.dot_general(
            both_ref[...], slab(0, start, size), dims, preferred_element_type=f32
        )
        rest = lax.dot_general(
            both_ref[:n, :], slab(1, start, size), dims, preferred_element_type=f32
        )
        return part[:n] + (part[n:] + rest)

    width = parts.shape[2 - dim]
    if by_rows:
        size = width // len(outs)
        for k, out in enumerate(outs):
            at = pl.multiple_of((place_ref[1] ^ k) * size, size)
            out[...] = multiply(at, size)
    else:
        size = min(512, width)
        piece = n // len(outs)
        for start in range(0, width, size):
            got = multiply(start, size)
            for k, out in enumerate(outs):
                out[:, start : start + size] = got[k * piece : (k + 1) * piece]


def product(place, ins, parts, dim, block, pieces, by_rows=False, span=None):
    spans = [span or (0, x.shape[0]) for x in ins]
    n = sum(end - start for start, end in spans)
    depth = ins[0].shape[1]
    width = parts.shape[2 - dim]
    shape = (n, width // pieces) if by_rows else (n // pieces, width)
    return pl.pallas_call(
        functools.partial(
            product_kernel, spans=spans, dim=dim, block=block, by_rows=by_rows
        ),
        out_shape=[jax.ShapeDtypeStruct(shape, f32)] * pieces,
        in_specs=[SMEM] + [VMEM] * (len(ins) + 1),
        out_specs=[VMEM] * pieces,
        scratch_shapes=[pltpu.VMEM((n, depth), f32), pltpu.VMEM((2 * n, depth), jnp.bfloat16)],
        compiler_params=LIMIT,
        name="product_rows" if by_rows else f"product_{dim}",
    )(place, *ins, parts)


def coefficients_kernel(place_ref, *refs, block, width, count):
    *ins, out_ref, all_ref = refs
    mask = place_ref[0]
    nparts = len(ins) // (2 * count)
    for c in range(count):
        firsts = ins[2 * c * nparts : (2 * c + 1) * nparts]
        seconds = ins[(2 * c + 1) * nparts : (2 * c + 2) * nparts]
        v = 0
        for f, s in zip(firsts, seconds):
            for i in range(0, f.shape[0], block):
                u = (v ^ mask) * block
                part = width // count
                at = (u // part) * width + c * part + u % part
                at = pl.multiple_of(at, block)
                all_ref[pl.ds(at, block), :] = f[i : i + block, :] + s[i : i + block, :]
                v += 1
    size = min(512, out_ref.shape[0])
    for start in range(0, out_ref.shape[0], size):
        out_ref[start : start + size, :] = all_ref[:, start : start + size].T


def coefficients_of(place, pairs, block, width):
    ins = [x for first, second in pairs for x in (*first, *second)]
    n = sum(x.shape[0] for x in ins) // 2
    depth = ins[0].shape[1]
    return pl.pallas_call(
        functools.partial(coefficients_kernel, block=block, width=width, count=len(pairs)),
        out_shape=jax.ShapeDtypeStruct((depth, n), f32),
        in_specs=[SMEM] + [VMEM] * len(ins),
        out_specs=VMEM,
        scratch_shapes=[pltpu.VMEM((n, depth), f32)],
        compiler_params=LIMIT,
        name="coefficients",
    )(place, *ins)


def send_half(x, axis, k, dim):
    half = x.shape[dim] // 2
    bit = (lax.axis_index(axis) // k) % 2
    return swap(lax.dynamic_slice_in_dim(x, (1 - bit) * half, half, dim), axis, k)


def keep_half(x, got, axis, k, dim):
    half = x.shape[dim] // 2
    bit = (lax.axis_index(axis) // k) % 2
    return lax.dynamic_slice_in_dim(x, bit * half, half, dim) + got


def join(x, got, axis, k, dim):
    bit = (lax.axis_index(axis) // k) % 2 == 1
    return jnp.concatenate([jnp.where(bit, got, x), jnp.where(bit, x, got)], dim)


def send_pieces(x, axis, dim):
    n = lax.axis_size(axis)
    me = lax.axis_index(axis)
    piece = x.shape[dim] // n
    return [
        swap(lax.dynamic_slice_in_dim(x, (me ^ k) * piece, piece, dim), axis, k)
        for k in range(1, n)
    ]


def keep_piece(x, got, axis, dim):
    piece = x.shape[dim] // lax.axis_size(axis)
    total = lax.dynamic_slice_in_dim(x, lax.axis_index(axis) * piece, piece, dim)
    for g in got:
        total = total + g
    return total


def send_all(x, axis):
    return [swap(x, axis, k) for k in range(1, lax.axis_size(axis))]


def join_all(x, got, axis, dim):
    n = lax.axis_size(axis)
    me = lax.axis_index(axis)
    got = [x] + got
    for k in bits(n):
        bit = (me // k) % 2 == 1
        got = [jnp.where(bit, got[j ^ k], got[j]) for j in range(n)]
    return jnp.concatenate(got, dim)


def all_sum(x):
    x = keep_half(x, send_half(x, "dom", 1, 0), "dom", 1, 0)
    x = keep_piece(x, send_pieces(x, "band", 0), "band", 0)
    total = x
    for k in range(1, lax.axis_size("dom") // 2):
        total = total + swap(x, "dom", 2 * k)
    x = join_all(total, send_all(total, "band"), "band", 0)
    return join(x, swap(x, "dom", 1), "dom", 1, 0)


class Order:
    def __init__(self):
        self.last = ()

    def after(self, *xs):
        got = lax.optimization_barrier((xs, self.last))[0]
        return got if len(got) > 1 else got[0]

    def done(self, *xs):
        self.last = xs


def sweep(order, whole, span, parts, masks, last):
    nband, ndom = lax.axis_size("band"), lax.axis_size("dom")
    to_dom, to_band, to_columns = masks
    n = (span[1] - span[0]) * nband
    block = n // ndom
    keep, send = product(to_dom, whole, parts, 0, block, 2, span=span)
    got = swap(send, "dom", 1)
    order.done(keep)
    yield None
    keep, got = order.after(keep, got)
    mine = [keep[i : i + block] + got[i : i + block] for i in range(0, n // 2, block)]
    got = [swap(mine[k], "dom", 2 * k) for k in range(1, ndom // 2)]
    order.done(*mine)
    yield None
    mine, *got = order.after(mine[0], *got)
    for g in got:
        mine = mine + g
    got = [swap(mine, "dom", 2 * k) for k in range(1, ndom // 2)]
    order.done(mine)
    yield None
    half = jnp.concatenate(order.after(mine, *got), 0)
    got = swap(half, "dom", 1)
    order.done(half)
    yield None
    coef = order.after(half, got)
    if last:
        terms = product(to_columns, coef, parts, 1, block, nband, by_rows=True)
    else:
        terms = product(to_band, coef, parts, 1, block, nband)
    got = [swap(terms[k], "band", k) for k in range(1, nband)]
    order.done(*terms)
    yield None
    total, *got = order.after(terms[0], *got)
    for g in got:
        total = total + g
    yield coef, total


def chunk(order, whole, span, parts, masks):
    whole = order.after(*whole)
    for out in sweep(order, whole, span, parts, masks, False):
        if out is None:
            yield None
    first, terms = out
    own = whole[0][span[0] : span[1]] - terms
    got = send_all(own, "band")
    order.done(own)
    yield None
    once = order.after(own, *got)
    for out in sweep(order, once, (0, own.shape[0]), parts, masks, True):
        if out is None:
            yield None
    second, terms = out
    rows = terms.shape[1]
    start = lax.axis_index("band") * rows
    mine = [lax.dynamic_slice_in_dim(o, start, rows, 1) for o in once]
    yield (first, second), join_all(mine[0], mine[1:], "band", 0) - terms


def mm(a, b, ca, cb):
    dims = (((ca,), (cb,)), ((), ()))
    return lax.dot_general(
        a, b, dims, precision=lax.Precision.HIGHEST, preferred_element_type=f32
    )


def small_factor(square, group):
    s = square.shape[0]
    n = 2 * s
    eye = lax.broadcasted_iota(jnp.int32, (s, s), 0) == lax.broadcasted_iota(jnp.int32, (s, s), 1)
    full = jnp.concatenate([square, jnp.where(eye, 1.0, 0.0).astype(f32)], 1)
    rid = lax.broadcasted_iota(jnp.int32, (s, n), 0)
    lid = lax.broadcasted_iota(jnp.int32, (s, n), 1)

    def tall(x):
        return jnp.concatenate([x] * (s // 8), 0)

    for j in range(0, s, group):
        cols = [jnp.broadcast_to(full[:, j + a : j + a + 1], (s, n)) for a in range(group)]
        rows = [jnp.broadcast_to(full[j + a : j + a + 1, :], (8, n)) for a in range(group)]
        pivots = [
            [jnp.broadcast_to(cols[b][j + a : j + a + 1, :], (8, n)) for b in range(group)]
            for a in range(group)
        ]
        for a in range(group):
            inv = 1.0 / pivots[a][a]
            for r in range(a + 1, group):
                m = pivots[r][a] * inv
                for c in range(a + 1, group):
                    pivots[r][c] = pivots[r][c] - m * pivots[a][c]
                rows[r] = rows[r] - m * rows[a]
            factor = jnp.where(rid > j + a, cols[a] * tall(inv), 0.0)
            for c in range(a + 1, group):
                cols[c] = cols[c] - factor * tall(pivots[a][c])
            full = full - factor * tall(rows[a])
    diag = jnp.sum(jnp.where(rid == lid, full, 0.0), axis=1, keepdims=True)
    root = lax.rsqrt(diag)
    root = root * (1.5 - 0.5 * diag * root * root)
    return full[:, s:] * root


def factor_kernel(gram_ref, out_ref, rest_ref, *, scale, size, group):
    n = gram_ref.shape[0]
    rest_ref[...] = gram_ref[...] * scale
    eye = lax.broadcasted_iota(jnp.int32, (n, n), 0) == lax.broadcasted_iota(jnp.int32, (n, n), 1)
    out_ref[...] = jnp.where(eye, 1.0, 0.0).astype(f32)
    for p in range(0, n, size):
        e = p + size
        x = small_factor(rest_ref[p:e, p:e], group)
        y = mm(x, out_ref[p:e, :], 1, 0)
        if e < n:
            w = mm(x, rest_ref[p:e, :], 1, 0)
            below = w[:, e:]
            rest_ref[e:, :] = rest_ref[e:, :] - mm(below, w, 0, 0)
            out_ref[e:, :] = out_ref[e:, :] - mm(below, y, 0, 0)
        out_ref[p:e, :] = y


def inverse_factor(gram, scale):
    n = gram.shape[0]
    return pl.pallas_call(
        functools.partial(factor_kernel, scale=scale, size=64, group=8),
        out_shape=jax.ShapeDtypeStruct((n, n), f32),
        in_specs=[pl.BlockSpec(memory_space=pltpu.VMEM)],
        out_specs=pl.BlockSpec(memory_space=pltpu.VMEM),
        scratch_shapes=[pltpu.VMEM((n, n), f32)],
        compiler_params=pltpu.CompilerParams(vmem_limit_bytes=16 << 20),
        name="inverse_factor",
    )(gram)


def shards(block, locked):
    width = block.shape[1]
    part = width // CHUNKS
    nband = lax.axis_size("band")
    total_rows = block.shape[0] * lax.axis_size("dom")
    own = block.T
    dom, band, ndom = lax.axis_index("dom"), lax.axis_index("band"), lax.axis_size("dom")
    by_dom = (dom % 2) * (ndom // 2) + dom // 2
    by_band = band * (ndom // nband)
    masks = [
        jnp.stack([m, band]).astype(jnp.int32)
        for m in (by_dom ^ by_band, by_dom ^ by_band, by_dom)
    ]
    parts = split_array(locked)
    order = Order()
    blocks = [own] + send_all(own, "band")
    spans = [(c * part, (c + 1) * part) for c in range(CHUNKS)]
    runs = [chunk(order, blocks, span, parts, masks) for span in spans]
    out = [None] * CHUNKS
    for c in TURNS:
        out["AB".index(c)] = next(runs["AB".index(c)])
    sums, twice = zip(*out)

    def ordered(xs):
        return jnp.concatenate(
            [x[b * part : (b + 1) * part] for b in range(nband) for x in xs], 0
        )

    mine = ordered(twice)
    block_rows = part * nband // ndom

    gram = all_sum(mm(mine, mine, 1, 1))
    coefficients = coefficients_of(masks[2], sums, block_rows, width)
    whole = join_all(mine, send_all(mine, "band"), "band", 1)
    inverse = inverse_factor(gram, 1.0 / total_rows)
    own_rows = lax.dynamic_slice_in_dim(inverse, lax.axis_index("band") * width, width, 0)
    basis = mm(own_rows, whole, 1, 0).T
    return (basis, coefficients)


def solution(mesh):
    placed = (P("dom", "band"), P("dom", "band"))
    return jax.shard_map(
        shards,
        mesh=mesh,
        in_specs=placed,
        out_specs=(P("dom", "band"), P("band", None)),
        check_vma=False,
    )
```

profile of v0, /device:TPU:0, one launch (start us, length us, event | category | flops | bytes accessed | tf_op | source)
XLA Modules:
  0.0 268.1 jit_solution(8690943179278115505)
XLA Ops:
  5.2 5.8 %copy-done.4 = f32[2048,2048]{1,0:T(8,128)S(1)} copy-done((f32[2048,2048]{1,0:T(8,128)S(1)}, f32[2048,2048]{1,0:T(8,128)}, u32[]{:S(2)}) %copy-start.4) | copy-done | bytes 16777240
  14.7 5.8 %copy-done = bf16[2,2048,2048]{2,1,0:T(8,128)(2,1)} copy-done((bf16[2,2048,2048]{2,1,0:T(8,128)(2,1)}, bf16[2,2048,2048]{2,1,0:T(8,128)(2,1)S(1)}, u32[]{:S(2)}) %copy-start) | copy-done | bytes 16777240
  20.5 7.4 %collective-permute-done.1.refs_2_ = f32[64,2048]{1,0:T(8,128)S(1)} collective-permute-done((f32[64,2048]{1,0:T(8,128)}, f32[64,2048]{1,0:T(8,128)S(1)}, u32[]{:S(2)}, u32[]{:S(2)}) %collective-permute-start.1) | collective-permute-done | bytes 524320 | tf_op jit(solution)/shard_map/ppermute | solution.py:17
  28.3 5.8 %copy-done.1 = bf16[2,2048,2048]{2,1,0:T(8,128)(2,1)S(1)} copy-done((bf16[2,2048,2048]{2,1,0:T(8,128)(2,1)S(1)}, bf16[2,2048,2048]{2,1,0:T(8,128)(2,1)}, u32[]{:S(2)}) %copy-start.1) | copy-done | bytes 16777240
  34.0 4.1 %product_0.4 = (f32[64,2048]{1,0:T(8,128)S(1)}, f32[64,2048]{1,0:T(8,128)S(1)}) custom-call(s32[2]{0:T(128)S(1)} %get-tuple-element.247.place_ref, f32[64,2048]{1,0:T(8,128)S(1)} %bitcast.9, f32[64,2048]{1,0:T(8,128)S(1)} %collective-permute-done.refs_1_, f32[64,2048]{1,0:T(8,128)S(1)} %collective-permute-done.1.refs_2_, ...), custom_call_target="tpu_custom_call" | custom-call | tf_op jit(solution)/shard_map/product_0/pallas_call | solution.py:122
  48.5 6.7 %collective-permute-done.5 = f32[16,2048]{1,0:T(8,128)S(1)} collective-permute-done((f32[16,2048]{1,0:T(8,128)S(1)}, f32[16,2048]{1,0:T(8,128)S(1)}, u32[]{:S(2)}, u32[]{:S(2)}) %collective-permute-start.5) | collective-permute-done | bytes 131104 | tf_op jit(solution)/shard_map/ppermute | solution.py:17
  59.7 4.1 %product_0.5 = (f32[64,2048]{1,0:T(8,128)S(1)}, f32[64,2048]{1,0:T(8,128)S(1)}) custom-call(s32[2]{0:T(128)S(1)} %get-tuple-element.247.place_ref, f32[64,2048]{1,0:T(8,128)S(1)} %bitcast.10, f32[64,2048]{1,0:T(8,128)S(1)} %collective-permute-done.refs_1_, f32[64,2048]{1,0:T(8,128)S(1)} %collective-permute-done.1.refs_2_, ...), custom_call_target="tpu_custom_call" | custom-call | tf_op jit(solution)/shard_map/product_0/pallas_call | solution.py:122
  63.9 4.1 %collective-permute-done.8 = f32[16,2048]{1,0:T(8,128)S(1)} collective-permute-done((f32[16,2048]{1,0:T(8,128)S(1)}, f32[16,2048]{1,0:T(8,128)S(1)}, u32[]{:S(2)}, u32[]{:S(2)}) %collective-permute-start.8) | collective-permute-done | bytes 131104 | tf_op jit(solution)/shard_map/ppermute | solution.py:17
  72.7 5.6 %product_1.2 = (f32[32,2048]{1,0:T(8,128)S(1)}, f32[32,2048]{1,0:T(8,128)S(1)}, f32[32,2048]{1,0:T(8,128)S(1)}, f32[32,2048]{1,0:T(8,128)S(1)}) custom-call(s32[2]{0:T(128)S(1)} %get-tuple-element.247.place_ref, f32[64,2048]{1,0:T(8,128)S(1)} %constant_dynamic-update-slice_fusion.refs_0_, f32[64,2048]{1,0:T(8,128)S(1)} %collective-permute-done.10.refs_1_, ...), custom_call_target="tpu_custom_call" | custom-call | tf_op jit(solution)/shard_map/product_1/pallas_call | solution.py:122
  87.6 5.5 %collective-permute-done.13 = f32[32,2048]{1,0:T(8,128)S(1)} collective-permute-done((f32[32,2048]{1,0:T(8,128)S(1)}, f32[32,2048]{1,0:T(8,128)S(1)}, u32[]{:S(2)}, u32[]{:S(2)}) %collective-permute-start.13) | collective-permute-done | bytes 262176 | tf_op jit(solution)/shard_map/ppermute | solution.py:17
  96.9 6.5 %collective-permute-done.20.refs_3_ = f32[32,2048]{1,0:T(8,128)S(1)} collective-permute-done((f32[32,2048]{1,0:T(8,128)S(1)}, f32[32,2048]{1,0:T(8,128)S(1)}, u32[]{:S(2)}, u32[]{:S(2)}) %collective-permute-start.20) | collective-permute-done | bytes 262176 | tf_op jit(solution)/shard_map/ppermute | solution.py:17
  106.4 4.3 %product_0.6 = (f32[64,2048]{1,0:T(8,128)S(1)}, f32[64,2048]{1,0:T(8,128)S(1)}) custom-call(s32[2]{0:T(128)S(1)} %get-tuple-element.247.place_ref, f32[32,2048]{1,0:T(8,128)S(1)} %add_subtract_fusion.1.refs_0_, f32[32,2048]{1,0:T(8,128)S(1)} %collective-permute-done.18.refs_1_, f32[32,2048]{1,0:T(8,128)S(1)} %collective-permute-done.19.refs_2_, ...), custom_call_target="tpu_custom_call" | custom-call | tf_op jit(solution)/shard_map/product_0/pallas_call | solution.py:122
  110.8 5.6 %product_1.3 = (f32[32,2048]{1,0:T(8,128)S(1)}, f32[32,2048]{1,0:T(8,128)S(1)}, f32[32,2048]{1,0:T(8,128)S(1)}, f32[32,2048]{1,0:T(8,128)S(1)}) custom-call(s32[2]{0:T(128)S(1)} %get-tuple-element.247.place_ref, f32[64,2048]{1,0:T(8,128)S(1)} %constant_dynamic-update-slice_fusion.4.refs_0_.refs_4_, f32[64,2048]{1,0:T(8,128)S(1)} %collective-permute-done.25.refs_1_.refs_5_, ...), custom_call_target="tpu_custom_call" | custom-call | tf_op jit(solution)/shard_map/product_1/pallas_call | solution.py:122
  126.2 5.1 %collective-permute-done.30 = f32[32,2048]{1,0:T(8,128)S(1)} collective-permute-done((f32[32,2048]{1,0:T(8,128)S(1)}, f32[32,2048]{1,0:T(8,128)S(1)}, u32[]{:S(2)}, u32[]{:S(2)}) %collective-permute-start.30) | collective-permute-done | bytes 262176 | tf_op jit(solution)/shard_map/ppermute | solution.py:17
  137.1 4.5 %collective-permute-done.37.refs_3_ = f32[32,2048]{1,0:T(8,128)S(1)} collective-permute-done((f32[32,2048]{1,0:T(8,128)S(1)}, f32[32,2048]{1,0:T(8,128)S(1)}, u32[]{:S(2)}, u32[]{:S(2)}) %collective-permute-start.37) | collective-permute-done | bytes 262176 | tf_op jit(solution)/shard_map/ppermute | solution.py:17
  145.4 4.1 %product_0.7 = (f32[64,2048]{1,0:T(8,128)S(1)}, f32[64,2048]{1,0:T(8,128)S(1)}) custom-call(s32[2]{0:T(128)S(1)} %get-tuple-element.247.place_ref, f32[32,2048]{1,0:T(8,128)S(1)} %add_subtract_fusion.refs_0_, f32[32,2048]{1,0:T(8,128)S(1)} %collective-permute-done.35.refs_1_, f32[32,2048]{1,0:T(8,128)S(1)} %collective-permute-done.36.refs_2_, ...), custom_call_target="tpu_custom_call" | custom-call | tf_op jit(solution)/shard_map/product_0/pallas_call | solution.py:122
  156.1 6.8 %product_rows.2 = (f32[128,512]{1,0:T(8,128)S(1)}, f32[128,512]{1,0:T(8,128)}, f32[128,512]{1,0:T(8,128)}, f32[128,512]{1,0:T(8,128)}) custom-call(s32[2]{0:T(128)S(1)} %get-tuple-element.248.place_ref, f32[64,2048]{1,0:T(8,128)S(1)} %constant_dynamic-update-slice_fusion.8.refs_0_.refs_2_, f32[64,2048]{1,0:T(8,128)S(1)} %collective-permute-done.38.refs_1_.refs_3_, ...), custom_call_target="tpu_custom_call" | custom-call | tf_op jit(solution)/shard_map/product_rows/pallas_call | solution.py:122
  183.6 4.0 %collective-permute-done.40 = f32[128,512]{1,0:T(8,128)} collective-permute-done((f32[128,512]{1,0:T(8,128)}, f32[128,512]{1,0:T(8,128)}, u32[]{:S(2)}, u32[]{:S(2)}) %collective-permute-start.40) | collective-permute-done | bytes 262176 | tf_op jit(solution)/shard_map/ppermute | solution.py:17
  187.5 6.5 %collective-permute-done.41 = f32[128,512]{1,0:T(8,128)} collective-permute-done((f32[128,512]{1,0:T(8,128)}, f32[128,512]{1,0:T(8,128)}, u32[]{:S(2)}, u32[]{:S(2)}) %collective-permute-start.41) | collective-permute-done | bytes 262176 | tf_op jit(solution)/shard_map/ppermute | solution.py:17
  194.0 5.8 %copy-done.3 = bf16[2,2048,2048]{2,1,0:T(8,128)(2,1)S(1)} copy-done((bf16[2,2048,2048]{2,1,0:T(8,128)(2,1)S(1)}, bf16[2,2048,2048]{2,1,0:T(8,128)(2,1)}, u32[]{:S(2)}) %copy-start.3) | copy-done | bytes 16777240
  199.8 6.1 %product_rows.3 = (f32[128,512]{1,0:T(8,128)S(1)}, f32[128,512]{1,0:T(8,128)S(1)}, f32[128,512]{1,0:T(8,128)S(1)}, f32[128,512]{1,0:T(8,128)S(1)}) custom-call(s32[2]{0:T(128)S(1)} %get-tuple-element.248.place_ref, f32[64,2048]{1,0:T(8,128)S(1)} %constant_dynamic-update-slice_fusion.12.refs_0_.refs_6_, f32[64,2048]{1,0:T(8,128)} %collective-permute-done.49.refs_1_.refs_7_, ...), custom_call_target="tpu_custom_call" | custom-call | tf_op jit(solution)/shard_map/product_rows/pallas_call | solution.py:122
  210.7 4.5 %collective-permute-done.50 = f32[128,512]{1,0:T(8,128)S(1)} collective-permute-done((f32[128,512]{1,0:T(8,128)S(1)}, f32[128,512]{1,0:T(8,128)S(1)}, u32[]{:S(2)}, u32[]{:S(2)}) %collective-permute-start.50) | collective-permute-done | bytes 262176 | tf_op jit(solution)/shard_map/ppermute | solution.py:17
  215.2 4.3 %collective-permute-done.51 = f32[128,512]{1,0:T(8,128)S(1)} collective-permute-done((f32[128,512]{1,0:T(8,128)S(1)}, f32[128,512]{1,0:T(8,128)S(1)}, u32[]{:S(2)}, u32[]{:S(2)}) %collective-permute-start.51) | collective-permute-done | bytes 262176 | tf_op jit(solution)/shard_map/ppermute | solution.py:17
  249.1 11.7 %inverse_factor.1 = f32[256,256]{1,0:T(8,128)S(1)} custom-call(f32[256,256]{1,0:T(8,128)S(1)} %pad_maximum_fusion.gram_ref), custom_call_target="tpu_custom_call" | custom-call | tf_op jit(solution)/shard_map/inverse_factor/pallas_call | solution.py:362
  (210 shorter events, 132.1 us)
Async XLA Ops:
  0.6 19.9 %collective-permute-start.2 = (f32[64,2048]{1,0:T(8,128)}, f32[64,2048]{1,0:T(8,128)S(1)}, u32[]{:S(2)}, u32[]{:S(2)}) collective-permute-start(f32[64,2048]{1,0:T(8,128)} %bitcast.6), channel_id=1, source_target_pairs={{0,3},{1,2},{2,1},{3,0},{4,7},{5,6},{6,5},{7,4},{8,11},{9,10},{10,... | collective-permute-start | bytes 1572872 | tf_op jit(solution)/shard_map/ppermute | solution.py:17
  4.6 23.4 %collective-permute-start.1 = (f32[64,2048]{1,0:T(8,128)}, f32[64,2048]{1,0:T(8,128)S(1)}, u32[]{:S(2)}, u32[]{:S(2)}) collective-permute-start(f32[64,2048]{1,0:T(8,128)} %bitcast.7), channel_id=1, source_target_pairs={{0,2},{1,3},{2,0},{3,1},{4,6},{5,7},{6,4},{7,5},{8,10},{9,11},{10,... | collective-permute-start | bytes 1572872 | tf_op jit(solution)/shard_map/ppermute | solution.py:17
  5.1 23.2 %collective-permute-start = (f32[64,2048]{1,0:T(8,128)}, f32[64,2048]{1,0:T(8,128)S(1)}, u32[]{:S(2)}, u32[]{:S(2)}) collective-permute-start(f32[64,2048]{1,0:T(8,128)} %bitcast.8), channel_id=1, source_target_pairs={{0,1},{1,0},{2,3},{3,2},{4,5},{5,4},{6,7},{7,6},{8,9},{9,8},{10,11... | collective-permute-start | bytes 1572872 | tf_op jit(solution)/shard_map/ppermute | solution.py:17
  68.2 12.3 %collective-permute-start.17 = (f32[16,2048]{1,0:T(8,128)S(1)}, f32[16,2048]{1,0:T(8,128)S(1)}, u32[]{:S(2)}, u32[]{:S(2)}) collective-permute-start(f32[16,2048]{1,0:T(8,128)S(1)} %get-tuple-element.230), channel_id=1, source_target_pairs={{0,24},{4,28},{8,16},{12,20},{16,8},{20,12},{24,0},{28,4},{1,25},{... | collective-permute-start | bytes 393224 | tf_op jit(solution)/shard_map/ppermute | solution.py:17
  79.9 13.2 %collective-permute-start.13 = (f32[32,2048]{1,0:T(8,128)S(1)}, f32[32,2048]{1,0:T(8,128)S(1)}, u32[]{:S(2)}, u32[]{:S(2)}) collective-permute-start(f32[32,2048]{1,0:T(8,128)S(1)} %get-tuple-element.134), channel_id=1, source_target_pairs={{0,2},{1,3},{2,0},{3,1},{4,6},{5,7},{6,4},{7,5},{8,10},{9,11},{10,... | collective-permute-start | bytes 786440 | tf_op jit(solution)/shard_map/ppermute | solution.py:17
  80.6 12.5 %collective-permute-start.14 = (f32[32,2048]{1,0:T(8,128)S(1)}, f32[32,2048]{1,0:T(8,128)S(1)}, u32[]{:S(2)}, u32[]{:S(2)}) collective-permute-start(f32[32,2048]{1,0:T(8,128)S(1)} %get-tuple-element.135), channel_id=1, source_target_pairs={{0,3},{1,2},{2,1},{3,0},{4,7},{5,6},{6,5},{7,4},{8,11},{9,10},{10,... | collective-permute-start | bytes 786440 | tf_op jit(solution)/shard_map/ppermute | solution.py:17
  82.3 12.9 %collective-permute-start.23 = (f32[16,2048]{1,0:T(8,128)S(1)}, f32[16,2048]{1,0:T(8,128)S(1)}, u32[]{:S(2)}, u32[]{:S(2)}) collective-permute-start(f32[16,2048]{1,0:T(8,128)S(1)} %add_add_fusion.2), channel_id=1, source_target_pairs={{0,24},{4,28},{8,16},{12,20},{16,8},{20,12},{24,0},{28,4},{1,25},{... | collective-permute-start | bytes 393224 | tf_op jit(solution)/shard_map/ppermute | solution.py:17
  83.9 12.8 %collective-permute-start.22 = (f32[16,2048]{1,0:T(8,128)S(1)}, f32[16,2048]{1,0:T(8,128)S(1)}, u32[]{:S(2)}, u32[]{:S(2)}) collective-permute-start(f32[16,2048]{1,0:T(8,128)S(1)} %add_add_fusion.2), channel_id=1, source_target_pairs={{0,16},{4,20},{8,24},{12,28},{16,0},{20,4},{24,8},{28,12},{1,17},{... | collective-permute-start | bytes 393224 | tf_op jit(solution)/shard_map/ppermute | solution.py:17
  96.8 14.0 %collective-permute-start.25 = (f32[64,2048]{1,0:T(8,128)S(1)}, f32[64,2048]{1,0:T(8,128)S(1)}, u32[]{:S(2)}, u32[]{:S(2)}) collective-permute-start(f32[64,2048]{1,0:T(8,128)S(1)} %constant_dynamic-update-slice_fusion.4.refs_0_.refs_4_), channel_id=1, source_target_pairs={{0,4},{4,0},{8,12},{12,8},{16,20},{20,16},{24,28},{28,24},{1,5},{5... | collective-permute-start | bytes 1572872 | tf_op jit(solution)/shard_map/ppermute | solution.py:17
  117.3 14.0 %collective-permute-start.30 = (f32[32,2048]{1,0:T(8,128)S(1)}, f32[32,2048]{1,0:T(8,128)S(1)}, u32[]{:S(2)}, u32[]{:S(2)}) collective-permute-start(f32[32,2048]{1,0:T(8,128)S(1)} %get-tuple-element.158), channel_id=1, source_target_pairs={{0,2},{1,3},{2,0},{3,1},{4,6},{5,7},{6,4},{7,5},{8,10},{9,11},{10,... | collective-permute-start | bytes 786440 | tf_op jit(solution)/shard_map/ppermute | solution.py:17
  118.5 12.7 %collective-permute-start.31 = (f32[32,2048]{1,0:T(8,128)S(1)}, f32[32,2048]{1,0:T(8,128)S(1)}, u32[]{:S(2)}, u32[]{:S(2)}) collective-permute-start(f32[32,2048]{1,0:T(8,128)S(1)} %get-tuple-element.159), channel_id=1, source_target_pairs={{0,3},{1,2},{2,1},{3,0},{4,7},{5,6},{6,5},{7,4},{8,11},{9,10},{10,... | collective-permute-start | bytes 786440 | tf_op jit(solution)/shard_map/ppermute | solution.py:17
  120.0 14.1 %collective-permute-start.28 = (f32[16,2048]{1,0:T(8,128)S(1)}, f32[16,2048]{1,0:T(8,128)S(1)}, u32[]{:S(2)}, u32[]{:S(2)}) collective-permute-start(f32[16,2048]{1,0:T(8,128)S(1)} %get-tuple-element.222), channel_id=1, source_target_pairs={{0,24},{4,28},{8,16},{12,20},{16,8},{20,12},{24,0},{28,4},{1,25},{... | collective-permute-start | bytes 393224 | tf_op jit(solution)/shard_map/ppermute | solution.py:17
  122.1 12.9 %collective-permute-start.27 = (f32[16,2048]{1,0:T(8,128)S(1)}, f32[16,2048]{1,0:T(8,128)S(1)}, u32[]{:S(2)}, u32[]{:S(2)}) collective-permute-start(f32[16,2048]{1,0:T(8,128)S(1)} %get-tuple-element.223), channel_id=1, source_target_pairs={{0,16},{4,20},{8,24},{12,28},{16,0},{20,4},{24,8},{28,12},{1,17},{... | collective-permute-start | bytes 393224 | tf_op jit(solution)/shard_map/ppermute | solution.py:17
  132.7 12.7 %collective-permute-start.36 = (f32[32,2048]{1,0:T(8,128)S(1)}, f32[32,2048]{1,0:T(8,128)S(1)}, u32[]{:S(2)}, u32[]{:S(2)}) collective-permute-start(f32[32,2048]{1,0:T(8,128)S(1)} %add_subtract_fusion.refs_0_), channel_id=1, source_target_pairs={{0,2},{1,3},{2,0},{3,1},{4,6},{5,7},{6,4},{7,5},{8,10},{9,11},{10,... | collective-permute-start | bytes 786440 | tf_op jit(solution)/shard_map/ppermute | solution.py:17
  135.0 14.7 %collective-permute-start.34 = (f32[16,2048]{1,0:T(8,128)S(1)}, f32[16,2048]{1,0:T(8,128)S(1)}, u32[]{:S(2)}, u32[]{:S(2)}) collective-permute-start(f32[16,2048]{1,0:T(8,128)S(1)} %add_add_fusion.1), channel_id=1, source_target_pairs={{0,24},{4,28},{8,16},{12,20},{16,8},{20,12},{24,0},{28,4},{1,25},{... | collective-permute-start | bytes 393224 | tf_op jit(solution)/shard_map/ppermute | solution.py:17
  137.0 12.6 %collective-permute-start.33 = (f32[16,2048]{1,0:T(8,128)S(1)}, f32[16,2048]{1,0:T(8,128)S(1)}, u32[]{:S(2)}, u32[]{:S(2)}) collective-permute-start(f32[16,2048]{1,0:T(8,128)S(1)} %add_add_fusion.1), channel_id=1, source_target_pairs={{0,16},{4,20},{8,24},{12,28},{16,0},{20,4},{24,8},{28,12},{1,17},{... | collective-permute-start | bytes 393224 | tf_op jit(solution)/shard_map/ppermute | solution.py:17
  153.6 12.0 %collective-permute-start.44 = (f32[16,2048]{1,0:T(8,128)S(1)}, f32[16,2048]{1,0:T(8,128)S(1)}, u32[]{:S(2)}, u32[]{:S(2)}) collective-permute-start(f32[16,2048]{1,0:T(8,128)S(1)} %get-tuple-element.219), channel_id=1, source_target_pairs={{0,16},{4,20},{8,24},{12,28},{16,0},{20,4},{24,8},{28,12},{1,17},{... | collective-permute-start | bytes 393224 | tf_op jit(solution)/shard_map/ppermute | solution.py:17
  178.0 16.0 %collective-permute-start.49 = (f32[64,2048]{1,0:T(8,128)S(1)}, f32[64,2048]{1,0:T(8,128)}, u32[]{:S(2)}, u32[]{:S(2)}) collective-permute-start(f32[64,2048]{1,0:T(8,128)S(1)} %constant_dynamic-update-slice_fusion.12.refs_0_.refs_6_), channel_id=1, source_target_pairs={{0,4},{4,0},{8,12},{12,8},{16,20},{20,16},{24,28},{28,24},{1,5},{5... | collective-permute-start | bytes 1572872 | tf_op jit(solution)/shard_map/ppermute | solution.py:17
  179.7 14.3 %collective-permute-start.41 = (f32[128,512]{1,0:T(8,128)}, f32[128,512]{1,0:T(8,128)}, u32[]{:S(2)}, u32[]{:S(2)}) collective-permute-start(f32[128,512]{1,0:T(8,128)} %get-tuple-element.186), channel_id=1, source_target_pairs={{0,2},{1,3},{2,0},{3,1},{4,6},{5,7},{6,4},{7,5},{8,10},{9,11},{10,... | collective-permute-start | bytes 786440 | tf_op jit(solution)/shard_map/ppermute | solution.py:17
  180.4 13.7 %collective-permute-start.42 = (f32[128,512]{1,0:T(8,128)}, f32[128,512]{1,0:T(8,128)}, u32[]{:S(2)}, u32[]{:S(2)}) collective-permute-start(f32[128,512]{1,0:T(8,128)} %get-tuple-element.187), channel_id=1, source_target_pairs={{0,3},{1,2},{2,1},{3,0},{4,7},{5,6},{6,5},{7,4},{8,11},{9,10},{10,... | collective-permute-start | bytes 786440 | tf_op jit(solution)/shard_map/ppermute | solution.py:17
  206.4 13.1 %collective-permute-start.51 = (f32[128,512]{1,0:T(8,128)S(1)}, f32[128,512]{1,0:T(8,128)S(1)}, u32[]{:S(2)}, u32[]{:S(2)}) collective-permute-start(f32[128,512]{1,0:T(8,128)S(1)} %get-tuple-element.204), channel_id=1, source_target_pairs={{0,2},{1,3},{2,0},{3,1},{4,6},{5,7},{6,4},{7,5},{8,10},{9,11},{10,... | collective-permute-start | bytes 786440 | tf_op jit(solution)/shard_map/ppermute | solution.py:17
  241.0 19.8 %collective-permute-start.55 = (f32[256,512]{1,0:T(8,128)}, f32[256,512]{1,0:T(8,128)}, u32[]{:S(2)}, u32[]{:S(2)}) collective-permute-start(f32[256,512]{1,0:T(8,128)} %copy-done.17), channel_id=1, source_target_pairs={{0,1},{1,0},{2,3},{3,2},{4,5},{5,4},{6,7},{7,6},{8,9},{9,8},{10,11... | collective-permute-start | bytes 1572872 | tf_op jit(solution)/shard_map/ppermute | solution.py:17
  241.4 22.5 %collective-permute-start.54 = (f32[256,512]{1,0:T(8,128)}, f32[256,512]{1,0:T(8,128)}, u32[]{:S(2)}, u32[]{:S(2)}) collective-permute-start(f32[256,512]{1,0:T(8,128)} %copy-done.17), channel_id=1, source_target_pairs={{0,2},{1,3},{2,0},{3,1},{4,6},{5,7},{6,4},{7,5},{8,10},{9,11},{10,... | collective-permute-start | bytes 1572872 | tf_op jit(solution)/shard_map/ppermute | solution.py:17
  242.9 21.0 %collective-permute-start.53 = (f32[256,512]{1,0:T(8,128)}, f32[256,512]{1,0:T(8,128)}, u32[]{:S(2)}, u32[]{:S(2)}) collective-permute-start(f32[256,512]{1,0:T(8,128)} %copy-done.17), channel_id=1, source_target_pairs={{0,3},{1,2},{2,1},{3,0},{4,7},{5,6},{6,5},{7,4},{8,11},{9,10},{10,... | collective-permute-start | bytes 1572872 | tf_op jit(solution)/shard_map/ppermute | solution.py:17
  (62 other events, 517.5 us)
where the time goes:
time: 271 us; the launch traced here: 268 us
  waiting for transfers between devices  100 us (37%)
  starting transfers between devices  71.6 us (26%)
  Pallas kernels  59.1 us (22%)
  local copies, waits for them, and re-layouts  26 us (10%)
  other arithmetic  6.59 us (2%)
  matrix products  2.9 us (1%)
    ppermute x67, waiting for transfers between devices, swap(): return lax.ppermute(x, axis, [(i, i ^ k) for i in range(n)])  100 us
    ppermute x67, starting transfers between devices, swap(): return lax.ppermute(x, axis, [(i, i ^ k) for i in range(n)])  71.6 us
    pallas_call x8, Pallas kernels, product(): pl.pallas_call(functools.partial(product_kernel, spans=spans, dim=dim, bl...  40.6 us
    unnamed x57, local copies, waits for them, and re-layouts  25.9 us
    pallas_call x1, Pallas kernels, inverse_factor(): pl.pallas_call(functools.partial(factor_kernel, scale=scale, size=64, gro...  11.7 us
  transfers between devices with their start and end apart: 67, of which 31 were waited for; matrix products, arithmetic and copies ran while one was open for 1% of the time, Pallas kernels for 18%

commit v1 on v0

--- a/solution.py
+++ b/solution.py
@@ -8,7 +8,7 @@
 from jax.sharding import PartitionSpec as P
 
 CHUNKS = 2
-TURNS = "AAABABABABABABABABABABBB"
+TURNS = "AAABABABABABABABABABBBAB"
 f32 = jnp.float32
 
 
@@ -23,8 +23,8 @@
 
 VMEM = pl.BlockSpec(memory_space=pltpu.VMEM)
 SMEM = pl.BlockSpec(memory_space=pltpu.SMEM)
-HBM = pl.BlockSpec(memory_space=pl.ANY)
-LIMIT = pltpu.CompilerParams(vmem_limit_bytes=8 << 20)
+HBM = pl.BlockSpec(memory_space=pltpu.HBM)
+LIMIT = pltpu.CompilerParams(vmem_limit_bytes=10 << 20)
 SLOTS = 4
 
 
@@ -33,7 +33,7 @@
     return high, (x - high.astype(f32)).astype(jnp.bfloat16)
 
 
-def split_kernel(x_ref, parts_ref, slots, sems):
+def split_kernel(x_ref, parts_ref, slots, halves, sems, outs):
     size = slots.shape[1]
     count = x_ref.shape[0] // size
 
@@ -42,27 +42,42 @@
             x_ref.at[pl.ds(i * size, size)], slots.at[i % SLOTS], sems.at[i % SLOTS]
         )
 
+    def back(i, which):
+        return pltpu.make_async_copy(
+            halves.at[i % SLOTS, which],
+            parts_ref.at[which, pl.ds(i * size, size)],
+            outs.at[i % SLOTS, which],
+        )
+
     for i in range(min(SLOTS, count)):
         copy(i).start()
     for i in range(count):
         copy(i).wait()
-        high, low = split(slots[i % SLOTS])
-        parts_ref[0, pl.ds(i * size, size), :] = high
-        parts_ref[1, pl.ds(i * size, size), :] = low
+        if i >= SLOTS:
+            back(i - SLOTS, 0).wait()
+            back(i - SLOTS, 1).wait()
+        halves[i % SLOTS, 0], halves[i % SLOTS, 1] = split(slots[i % SLOTS])
+        back(i, 0).start()
+        back(i, 1).start()
         if i + SLOTS < count:
             copy(i + SLOTS).start()
+    for i in range(max(count - SLOTS, 0), count):
+        back(i, 0).wait()
+        back(i, 1).wait()
 
 
 def split_array(x):
     size = 128
     return pl.pallas_call(
         split_kernel,
-        out_shape=jax.ShapeDtypeStruct((2, *x.shape), jnp.bfloat16),
+        out_shape=pltpu.HBM((2, *x.shape), jnp.bfloat16),
         in_specs=[HBM],
-        out_specs=VMEM,
+        out_specs=HBM,
         scratch_shapes=[
             pltpu.VMEM((SLOTS, size, x.shape[1]), f32),
+            pltpu.VMEM((SLOTS, 2, size, x.shape[1]), jnp.bfloat16),
             pltpu.SemaphoreType.DMA((SLOTS,)),
+            pltpu.SemaphoreType.DMA((SLOTS, 2)),
         ],
         compiler_params=LIMIT,
         name="split_array",
@@ -130,6 +145,22 @@
         compiler_params=LIMIT,
         name="product_rows" if by_rows else f"product_{dim}",
     )(place, *ins, parts)
+
+
+def touch_kernel(parts_ref, out_ref):
+    rows, columns = out_ref.shape
+    out_ref[...] = parts_ref[0, :rows, :columns].astype(f32)
+
+
+def touch(parts):
+    return pl.pallas_call(
+        touch_kernel,
+        out_shape=jax.ShapeDtypeStruct((16, 128), f32),
+        in_specs=[VMEM],
+        out_specs=VMEM,
+        compiler_params=LIMIT,
+        name="touch",
+    )(parts)
 
 
 def coefficients_kernel(place_ref, *refs, block, width, count):
@@ -160,10 +191,10 @@
     return pl.pallas_call(
         functools.partial(coefficients_kernel, block=block, width=width, count=len(pairs)),
         out_shape=jax.ShapeDtypeStruct((depth, n), f32),
-        in_specs=[SMEM] + [VMEM] * len(ins),
-        out_specs=VMEM,
+        in_specs=[SMEM] + [pl.BlockSpec(x.shape, lambda: (0, 0)) for x in ins],
+        out_specs=pl.BlockSpec((depth, n), lambda: (0, 0)),
         scratch_shapes=[pltpu.VMEM((n, depth), f32)],
-        compiler_params=LIMIT,
+        compiler_params=pltpu.CompilerParams(vmem_limit_bytes=16 << 20),
         name="coefficients",
     )(place, *ins)
 
@@ -387,6 +418,7 @@
     order = Order()
     blocks = [own] + send_all(own, "band")
     spans = [(c * part, (c + 1) * part) for c in range(CHUNKS)]
+    order.done(touch(parts))
     runs = [chunk(order, blocks, span, parts, masks) for span in spans]
     out = [None] * CHUNKS
     for c in TURNS:
@@ -402,9 +434,12 @@
     block_rows = part * nband // ndom
 
     gram = all_sum(mm(mine, mine, 1, 1))
-    coefficients = coefficients_of(masks[2], sums, block_rows, width)
     whole = join_all(mine, send_all(mine, "band"), "band", 1)
     inverse = inverse_factor(gram, 1.0 / total_rows)
+    flat = lax.optimization_barrier(([x for pair in sums for half in pair for x in half], inverse))[0]
+    taken = iter(flat)
+    pairs = [tuple(tuple(next(taken) for _ in half) for half in pair) for pair in sums]
+    coefficients = coefficients_of(masks[2], pairs, block_rows, width)
     own_rows = lax.dynamic_slice_in_dim(inverse, lax.axis_index("band") * width, width, 0)
     basis = mm(own_rows, whole, 1, 0).T
     return (basis, coefficients)

time: 271 us -> 262 us (0.967)
  waiting for transfers between devices: 100 us -> 93.4 us
  local copies, waits for them, and re-layouts: 26 us -> 20.2 us
    ppermute x67, waiting for transfers between devices: 100 us -> 93.4 us  [swap(): return lax.ppermute(x, axis, [(i, i ^ k) for i in range(n)])]
    unnamed x57 -> x55, local copies, waits for them, and re-layouts: 25.9 us -> 20.1 us
  transfers between devices with their start and end apart: 67 -> 67, of which waited for: 31 -> 31; matrix products, arithmetic and copies ran while one was open for 1% -> 2% of each run, Pallas kernels for 18% -> 22%
where the time goes in v1:
time: 262 us; the launch traced here: 259 us
  waiting for transfers between devices  93.4 us (36%)
  starting transfers between devices  71.5 us (27%)
  Pallas kernels  61.7 us (24%)
  local copies, waits for them, and re-layouts  20.2 us (8%)
  other arithmetic  7.46 us (3%)
  matrix products  2.9 us (1%)
    ppermute x67, waiting for transfers between devices, swap(): return lax.ppermute(x, axis, [(i, i ^ k) for i in range(n)])  93.4 us
    ppermute x67, starting transfers between devices, swap(): return lax.ppermute(x, axis, [(i, i ^ k) for i in range(n)])  71.5 us
    pallas_call x8, Pallas kernels, product(): pl.pallas_call(functools.partial(product_kernel, spans=spans, dim=dim, bl...  40.6 us
    unnamed x55, local copies, waits for them, and re-layouts  20.1 us
    pallas_call x1, Pallas kernels, inverse_factor(): pl.pallas_call(functools.partial(factor_kernel, scale=scale, size=64, gro...  11.7 us
    pallas_call x1, Pallas kernels, split_array(): pl.pallas_call(split_kernel, out_shape=pltpu.HBM((2, *x.shape), jnp.bfloa...  6.25 us
  transfers between devices with their start and end apart: 67, of which 31 were waited for; matrix products, arithmetic and copies ran while one was open for 2% of the time, Pallas kernels for 22%

profile of v1, /device:TPU:0, one launch (start us, length us, event | category | flops | bytes accessed | tf_op | source)
XLA Modules:
  0.0 258.7 jit_solution(727229360230934719)
XLA Ops:
  0.6 4.0 %collective-permute-start.2 = (f32[64,2048]{1,0:T(8,128)}, f32[64,2048]{1,0:T(8,128)S(1)}, u32[]{:S(2)}, u32[]{:S(2)}) collective-permute-start(f32[64,2048]{1,0:T(8,128)} %bitcast.6), channel_id=1, source_target_pairs={{0,3},{1,2},{2,1},{3,0},{4,7},{5,6},{6,5},{7,4},{8,11},{9,10},{10,... | collective-permute-start | bytes 1572872 | tf_op jit(solution)/shard_map/ppermute | solution.py:17
  5.2 5.8 %copy-done.3 = f32[2048,2048]{1,0:T(8,128)S(1)} copy-done((f32[2048,2048]{1,0:T(8,128)S(1)}, f32[2048,2048]{1,0:T(8,128)}, u32[]{:S(2)}) %copy-start.3) | copy-done | bytes 16777240
  11.0 6.3 %split_array.1.refs_4_.refs_2_ = bf16[2,2048,2048]{2,1,0:T(8,128)(2,1)} custom-call(f32[2048,2048]{1,0:T(8,128)S(1)} %copy-done.3), custom_call_target="tpu_custom_call" | custom-call | tf_op jit(solution)/shard_map/split_array/pallas_call | solution.py:71
  17.6 10.4 %collective-permute-done.1.refs_2_ = f32[64,2048]{1,0:T(8,128)S(1)} collective-permute-done((f32[64,2048]{1,0:T(8,128)}, f32[64,2048]{1,0:T(8,128)S(1)}, u32[]{:S(2)}, u32[]{:S(2)}) %collective-permute-start.1) | collective-permute-done | bytes 524320 | tf_op jit(solution)/shard_map/ppermute | solution.py:17
  28.3 5.8 %copy-done = bf16[2,2048,2048]{2,1,0:T(8,128)(2,1)S(1)} copy-done((bf16[2,2048,2048]{2,1,0:T(8,128)(2,1)S(1)}, bf16[2,2048,2048]{2,1,0:T(8,128)(2,1)}, u32[]{:S(2)}) %copy-start) | copy-done | bytes 16777240
  34.0 4.1 %product_0.4 = (f32[64,2048]{1,0:T(8,128)S(1)}, f32[64,2048]{1,0:T(8,128)S(1)}) custom-call(s32[2]{0:T(128)S(1)} %get-tuple-element.263.place_ref, f32[64,2048]{1,0:T(8,128)S(1)} %bitcast.9, f32[64,2048]{1,0:T(8,128)S(1)} %collective-permute-done.refs_1_, f32[64,2048]{1,0:T(8,128)S(1)} %collective-permute-done.1.refs_2_, ...), custom_call_target="tpu_custom_call" | custom-call | tf_op jit(solution)/shard_map/product_0/pallas_call | solution.py:137
  48.5 6.7 %collective-permute-done.5 = f32[16,2048]{1,0:T(8,128)S(1)} collective-permute-done((f32[16,2048]{1,0:T(8,128)S(1)}, f32[16,2048]{1,0:T(8,128)S(1)}, u32[]{:S(2)}, u32[]{:S(2)}) %collective-permute-start.5) | collective-permute-done | bytes 131104 | tf_op jit(solution)/shard_map/ppermute | solution.py:17
  59.7 4.1 %product_0.5 = (f32[64,2048]{1,0:T(8,128)S(1)}, f32[64,2048]{1,0:T(8,128)S(1)}) custom-call(s32[2]{0:T(128)S(1)} %get-tuple-element.263.place_ref, f32[64,2048]{1,0:T(8,128)S(1)} %bitcast.10, f32[64,2048]{1,0:T(8,128)S(1)} %collective-permute-done.refs_1_, f32[64,2048]{1,0:T(8,128)S(1)} %collective-permute-done.1.refs_2_, ...), custom_call_target="tpu_custom_call" | custom-call | tf_op jit(solution)/shard_map/product_0/pallas_call | solution.py:137
  63.9 4.1 %collective-permute-done.8 = f32[16,2048]{1,0:T(8,128)S(1)} collective-permute-done((f32[16,2048]{1,0:T(8,128)S(1)}, f32[16,2048]{1,0:T(8,128)S(1)}, u32[]{:S(2)}, u32[]{:S(2)}) %collective-permute-start.8) | collective-permute-done | bytes 131104 | tf_op jit(solution)/shard_map/ppermute | solution.py:17
  72.7 5.6 %product_1.2 = (f32[32,2048]{1,0:T(8,128)S(1)}, f32[32,2048]{1,0:T(8,128)S(1)}, f32[32,2048]{1,0:T(8,128)S(1)}, f32[32,2048]{1,0:T(8,128)S(1)}) custom-call(s32[2]{0:T(128)S(1)} %get-tuple-element.263.place_ref, f32[64,2048]{1,0:T(8,128)S(1)} %constant_dynamic-update-slice_fusion.refs_0_, f32[64,2048]{1,0:T(8,128)S(1)} %collective-permute-done.10.refs_1_, ...), custom_call_target="tpu_custom_call" | custom-call | tf_op jit(solution)/shard_map/product_1/pallas_call | solution.py:137
  87.6 5.5 %collective-permute-done.13 = f32[32,2048]{1,0:T(8,128)S(1)} collective-permute-done((f32[32,2048]{1,0:T(8,128)S(1)}, f32[32,2048]{1,0:T(8,128)S(1)}, u32[]{:S(2)}, u32[]{:S(2)}) %collective-permute-start.13) | collective-permute-done | bytes 262176 | tf_op jit(solution)/shard_map/ppermute | solution.py:17
  96.9 6.5 %collective-permute-done.20.refs_3_ = f32[32,2048]{1,0:T(8,128)S(1)} collective-permute-done((f32[32,2048]{1,0:T(8,128)S(1)}, f32[32,2048]{1,0:T(8,128)S(1)}, u32[]{:S(2)}, u32[]{:S(2)}) %collective-permute-start.20) | collective-permute-done | bytes 262176 | tf_op jit(solution)/shard_map/ppermute | solution.py:17
  106.4 4.3 %product_0.6 = (f32[64,2048]{1,0:T(8,128)S(1)}, f32[64,2048]{1,0:T(8,128)S(1)}) custom-call(s32[2]{0:T(128)S(1)} %get-tuple-element.263.place_ref, f32[32,2048]{1,0:T(8,128)S(1)} %add_subtract_fusion.1.refs_0_, f32[32,2048]{1,0:T(8,128)S(1)} %collective-permute-done.18.refs_1_, f32[32,2048]{1,0:T(8,128)S(1)} %collective-permute-done.19.refs_2_, ...), custom_call_target="tpu_custom_call" | custom-call | tf_op jit(solution)/shard_map/product_0/pallas_call | solution.py:137
  110.8 5.6 %product_1.3 = (f32[32,2048]{1,0:T(8,128)S(1)}, f32[32,2048]{1,0:T(8,128)S(1)}, f32[32,2048]{1,0:T(8,128)S(1)}, f32[32,2048]{1,0:T(8,128)S(1)}) custom-call(s32[2]{0:T(128)S(1)} %get-tuple-element.263.place_ref, f32[64,2048]{1,0:T(8,128)S(1)} %constant_dynamic-update-slice_fusion.4.refs_0_.refs_4_, f32[64,2048]{1,0:T(8,128)S(1)} %collective-permute-done.25.refs_1_.refs_5_, ...), custom_call_target="tpu_custom_call" | custom-call | tf_op jit(solution)/shard_map/product_1/pallas_call | solution.py:137
  126.1 5.1 %collective-permute-done.30 = f32[32,2048]{1,0:T(8,128)S(1)} collective-permute-done((f32[32,2048]{1,0:T(8,128)S(1)}, f32[32,2048]{1,0:T(8,128)S(1)}, u32[]{:S(2)}, u32[]{:S(2)}) %collective-permute-start.30) | collective-permute-done | bytes 262176 | tf_op jit(solution)/shard_map/ppermute | solution.py:17
  137.1 4.5 %collective-permute-done.37.refs_3_ = f32[32,2048]{1,0:T(8,128)S(1)} collective-permute-done((f32[32,2048]{1,0:T(8,128)S(1)}, f32[32,2048]{1,0:T(8,128)S(1)}, u32[]{:S(2)}, u32[]{:S(2)}) %collective-permute-start.37) | collective-permute-done | bytes 262176 | tf_op jit(solution)/shard_map/ppermute | solution.py:17
  145.4 4.1 %product_0.7 = (f32[64,2048]{1,0:T(8,128)S(1)}, f32[64,2048]{1,0:T(8,128)S(1)}) custom-call(s32[2]{0:T(128)S(1)} %get-tuple-element.263.place_ref, f32[32,2048]{1,0:T(8,128)S(1)} %add_subtract_fusion.refs_0_, f32[32,2048]{1,0:T(8,128)S(1)} %collective-permute-done.35.refs_1_, f32[32,2048]{1,0:T(8,128)S(1)} %collective-permute-done.36.refs_2_, ...), custom_call_target="tpu_custom_call" | custom-call | tf_op jit(solution)/shard_map/product_0/pallas_call | solution.py:137
  156.1 6.7 %product_rows.2 = (f32[128,512]{1,0:T(8,128)S(1)}, f32[128,512]{1,0:T(8,128)}, f32[128,512]{1,0:T(8,128)}, f32[128,512]{1,0:T(8,128)}) custom-call(s32[2]{0:T(128)S(1)} %get-tuple-element.264.place_ref, f32[64,2048]{1,0:T(8,128)S(1)} %constant_dynamic-update-slice_fusion.8.refs_0_.refs_2_, f32[64,2048]{1,0:T(8,128)S(1)} %collective-permute-done.38.refs_1_.refs_3_, ...), custom_call_target="tpu_custom_call" | custom-call | tf_op jit(solution)/shard_map/product_rows/pallas_call | solution.py:137
  170.2 3.9 %collective-permute-done.48 = f32[16,2048]{1,0:T(8,128)S(1)} collective-permute-done((f32[16,2048]{1,0:T(8,128)S(1)}, f32[16,2048]{1,0:T(8,128)S(1)}, u32[]{:S(2)}, u32[]{:S(2)}) %collective-permute-start.48) | collective-permute-done | bytes 131104 | tf_op jit(solution)/shard_map/ppermute | solution.py:17
  183.5 5.8 %copy-done.2 = bf16[2,2048,2048]{2,1,0:T(8,128)(2,1)S(1)} copy-done((bf16[2,2048,2048]{2,1,0:T(8,128)(2,1)S(1)}, bf16[2,2048,2048]{2,1,0:T(8,128)(2,1)}, u32[]{:S(2)}) %copy-start.2) | copy-done | bytes 16777240
  189.3 6.1 %product_rows.3 = (f32[128,512]{1,0:T(8,128)S(1)}, f32[128,512]{1,0:T(8,128)S(1)}, f32[128,512]{1,0:T(8,128)S(1)}, f32[128,512]{1,0:T(8,128)S(1)}) custom-call(s32[2]{0:T(128)S(1)} %get-tuple-element.264.place_ref, f32[64,2048]{1,0:T(8,128)S(1)} %constant_dynamic-update-slice_fusion.12.refs_0_.refs_6_, f32[64,2048]{1,0:T(8,128)} %collective-permute-done.49.refs_1_.refs_7_, ...), custom_call_target="tpu_custom_call" | custom-call | tf_op jit(solution)/shard_map/product_rows/pallas_call | solution.py:137
  200.3 4.5 %collective-permute-done.50 = f32[128,512]{1,0:T(8,128)S(1)} collective-permute-done((f32[128,512]{1,0:T(8,128)S(1)}, f32[128,512]{1,0:T(8,128)S(1)}, u32[]{:S(2)}, u32[]{:S(2)}) %collective-permute-start.50) | collective-permute-done | bytes 262176 | tf_op jit(solution)/shard_map/ppermute | solution.py:17
  204.7 5.5 %collective-permute-done.51 = f32[128,512]{1,0:T(8,128)S(1)} collective-permute-done((f32[128,512]{1,0:T(8,128)S(1)}, f32[128,512]{1,0:T(8,128)S(1)}, u32[]{:S(2)}, u32[]{:S(2)}) %collective-permute-start.51) | collective-permute-done | bytes 262176 | tf_op jit(solution)/shard_map/ppermute | solution.py:17
  237.0 11.7 %inverse_factor.1 = f32[256,256]{1,0:T(8,128)S(1)} custom-call(f32[256,256]{1,0:T(8,128)S(1)} %pad_maximum_fusion.gram_ref), custom_call_target="tpu_custom_call" | custom-call | tf_op jit(solution)/shard_map/inverse_factor/pallas_call | solution.py:393
  (208 shorter events, 120.8 us)
Async XLA Ops:
  0.6 17.0 %collective-permute-start.2 = (f32[64,2048]{1,0:T(8,128)}, f32[64,2048]{1,0:T(8,128)S(1)}, u32[]{:S(2)}, u32[]{:S(2)}) collective-permute-start(f32[64,2048]{1,0:T(8,128)} %bitcast.6), channel_id=1, source_target_pairs={{0,3},{1,2},{2,1},{3,0},{4,7},{5,6},{6,5},{7,4},{8,11},{9,10},{10,... | collective-permute-start | bytes 1572872 | tf_op jit(solution)/shard_map/ppermute | solution.py:17
  4.6 23.4 %collective-permute-start.1 = (f32[64,2048]{1,0:T(8,128)}, f32[64,2048]{1,0:T(8,128)S(1)}, u32[]{:S(2)}, u32[]{:S(2)}) collective-permute-start(f32[64,2048]{1,0:T(8,128)} %bitcast.7), channel_id=1, source_target_pairs={{0,2},{1,3},{2,0},{3,1},{4,6},{5,7},{6,4},{7,5},{8,10},{9,11},{10,... | collective-permute-start | bytes 1572872 | tf_op jit(solution)/shard_map/ppermute | solution.py:17
  5.1 23.2 %collective-permute-start = (f32[64,2048]{1,0:T(8,128)}, f32[64,2048]{1,0:T(8,128)S(1)}, u32[]{:S(2)}, u32[]{:S(2)}) collective-permute-start(f32[64,2048]{1,0:T(8,128)} %bitcast.8), channel_id=1, source_target_pairs={{0,1},{1,0},{2,3},{3,2},{4,5},{5,4},{6,7},{7,6},{8,9},{9,8},{10,11... | collective-permute-start | bytes 1572872 | tf_op jit(solution)/shard_map/ppermute | solution.py:17
  68.2 12.3 %collective-permute-start.17 = (f32[16,2048]{1,0:T(8,128)S(1)}, f32[16,2048]{1,0:T(8,128)S(1)}, u32[]{:S(2)}, u32[]{:S(2)}) collective-permute-start(f32[16,2048]{1,0:T(8,128)S(1)} %get-tuple-element.246), channel_id=1, source_target_pairs={{0,24},{4,28},{8,16},{12,20},{16,8},{20,12},{24,0},{28,4},{1,25},{... | collective-permute-start | bytes 393224 | tf_op jit(solution)/shard_map/ppermute | solution.py:17
  79.9 13.2 %collective-permute-start.13 = (f32[32,2048]{1,0:T(8,128)S(1)}, f32[32,2048]{1,0:T(8,128)S(1)}, u32[]{:S(2)}, u32[]{:S(2)}) collective-permute-start(f32[32,2048]{1,0:T(8,128)S(1)} %get-tuple-element.142), channel_id=1, source_target_pairs={{0,2},{1,3},{2,0},{3,1},{4,6},{5,7},{6,4},{7,5},{8,10},{9,11},{10,... | collective-permute-start | bytes 786440 | tf_op jit(solution)/shard_map/ppermute | solution.py:17
  80.6 12.5 %collective-permute-start.14 = (f32[32,2048]{1,0:T(8,128)S(1)}, f32[32,2048]{1,0:T(8,128)S(1)}, u32[]{:S(2)}, u32[]{:S(2)}) collective-permute-start(f32[32,2048]{1,0:T(8,128)S(1)} %get-tuple-element.143), channel_id=1, source_target_pairs={{0,3},{1,2},{2,1},{3,0},{4,7},{5,6},{6,5},{7,4},{8,11},{9,10},{10,... | collective-permute-start | bytes 786440 | tf_op jit(solution)/shard_map/ppermute | solution.py:17
  82.3 12.9 %collective-permute-start.23 = (f32[16,2048]{1,0:T(8,128)S(1)}, f32[16,2048]{1,0:T(8,128)S(1)}, u32[]{:S(2)}, u32[]{:S(2)}) collective-permute-start(f32[16,2048]{1,0:T(8,128)S(1)} %add_add_fusion.2), channel_id=1, source_target_pairs={{0,24},{4,28},{8,16},{12,20},{16,8},{20,12},{24,0},{28,4},{1,25},{... | collective-permute-start | bytes 393224 | tf_op jit(solution)/shard_map/ppermute | solution.py:17
  83.9 12.8 %collective-permute-start.22 = (f32[16,2048]{1,0:T(8,128)S(1)}, f32[16,2048]{1,0:T(8,128)S(1)}, u32[]{:S(2)}, u32[]{:S(2)}) collective-permute-start(f32[16,2048]{1,0:T(8,128)S(1)} %add_add_fusion.2), channel_id=1, source_target_pairs={{0,16},{4,20},{8,24},{12,28},{16,0},{20,4},{24,8},{28,12},{1,17},{... | collective-permute-start | bytes 393224 | tf_op jit(solution)/shard_map/ppermute | solution.py:17
  96.8 14.0 %collective-permute-start.25 = (f32[64,2048]{1,0:T(8,128)S(1)}, f32[64,2048]{1,0:T(8,128)S(1)}, u32[]{:S(2)}, u32[]{:S(2)}) collective-permute-start(f32[64,2048]{1,0:T(8,128)S(1)} %constant_dynamic-update-slice_fusion.4.refs_0_.refs_4_), channel_id=1, source_target_pairs={{0,4},{4,0},{8,12},{12,8},{16,20},{20,16},{24,28},{28,24},{1,5},{5... | collective-permute-start | bytes 1572872 | tf_op jit(solution)/shard_map/ppermute | solution.py:17
  117.2 14.0 %collective-permute-start.30 = (f32[32,2048]{1,0:T(8,128)S(1)}, f32[32,2048]{1,0:T(8,128)S(1)}, u32[]{:S(2)}, u32[]{:S(2)}) collective-permute-start(f32[32,2048]{1,0:T(8,128)S(1)} %get-tuple-element.166), channel_id=1, source_target_pairs={{0,2},{1,3},{2,0},{3,1},{4,6},{5,7},{6,4},{7,5},{8,10},{9,11},{10,... | collective-permute-start | bytes 786440 | tf_op jit(solution)/shard_map/ppermute | solution.py:17
  118.5 12.7 %collective-permute-start.31 = (f32[32,2048]{1,0:T(8,128)S(1)}, f32[32,2048]{1,0:T(8,128)S(1)}, u32[]{:S(2)}, u32[]{:S(2)}) collective-permute-start(f32[32,2048]{1,0:T(8,128)S(1)} %get-tuple-element.167), channel_id=1, source_target_pairs={{0,3},{1,2},{2,1},{3,0},{4,7},{5,6},{6,5},{7,4},{8,11},{9,10},{10,... | collective-permute-start | bytes 786440 | tf_op jit(solution)/shard_map/ppermute | solution.py:17
  120.0 14.1 %collective-permute-start.28 = (f32[16,2048]{1,0:T(8,128)S(1)}, f32[16,2048]{1,0:T(8,128)S(1)}, u32[]{:S(2)}, u32[]{:S(2)}) collective-permute-start(f32[16,2048]{1,0:T(8,128)S(1)} %get-tuple-element.238), channel_id=1, source_target_pairs={{0,24},{4,28},{8,16},{12,20},{16,8},{20,12},{24,0},{28,4},{1,25},{... | collective-permute-start | bytes 393224 | tf_op jit(solution)/shard_map/ppermute | solution.py:17
  122.0 12.9 %collective-permute-start.27 = (f32[16,2048]{1,0:T(8,128)S(1)}, f32[16,2048]{1,0:T(8,128)S(1)}, u32[]{:S(2)}, u32[]{:S(2)}) collective-permute-start(f32[16,2048]{1,0:T(8,128)S(1)} %get-tuple-element.239), channel_id=1, source_target_pairs={{0,16},{4,20},{8,24},{12,28},{16,0},{20,4},{24,8},{28,12},{1,17},{... | collective-permute-start | bytes 393224 | tf_op jit(solution)/shard_map/ppermute | solution.py:17
  132.7 12.7 %collective-permute-start.36 = (f32[32,2048]{1,0:T(8,128)S(1)}, f32[32,2048]{1,0:T(8,128)S(1)}, u32[]{:S(2)}, u32[]{:S(2)}) collective-permute-start(f32[32,2048]{1,0:T(8,128)S(1)} %add_subtract_fusion.refs_0_), channel_id=1, source_target_pairs={{0,2},{1,3},{2,0},{3,1},{4,6},{5,7},{6,4},{7,5},{8,10},{9,11},{10,... | collective-permute-start | bytes 786440 | tf_op jit(solution)/shard_map/ppermute | solution.py:17
  135.0 14.7 %collective-permute-start.34 = (f32[16,2048]{1,0:T(8,128)S(1)}, f32[16,2048]{1,0:T(8,128)S(1)}, u32[]{:S(2)}, u32[]{:S(2)}) collective-permute-start(f32[16,2048]{1,0:T(8,128)S(1)} %add_add_fusion.1), channel_id=1, source_target_pairs={{0,24},{4,28},{8,16},{12,20},{16,8},{20,12},{24,0},{28,4},{1,25},{... | collective-permute-start | bytes 393224 | tf_op jit(solution)/shard_map/ppermute | solution.py:17
  137.0 12.7 %collective-permute-start.33 = (f32[16,2048]{1,0:T(8,128)S(1)}, f32[16,2048]{1,0:T(8,128)S(1)}, u32[]{:S(2)}, u32[]{:S(2)}) collective-permute-start(f32[16,2048]{1,0:T(8,128)S(1)} %add_add_fusion.1), channel_id=1, source_target_pairs={{0,16},{4,20},{8,24},{12,28},{16,0},{20,4},{24,8},{28,12},{1,17},{... | collective-permute-start | bytes 393224 | tf_op jit(solution)/shard_map/ppermute | solution.py:17
  178.1 19.7 %collective-permute-start.40 = (f32[128,512]{1,0:T(8,128)}, f32[128,512]{1,0:T(8,128)}, u32[]{:S(2)}, u32[]{:S(2)}) collective-permute-start(f32[128,512]{1,0:T(8,128)} %get-tuple-element.193), channel_id=1, source_target_pairs={{0,1},{1,0},{2,3},{3,2},{4,5},{5,4},{6,7},{7,6},{8,9},{9,8},{10,11... | collective-permute-start | bytes 786440 | tf_op jit(solution)/shard_map/ppermute | solution.py:17
  179.7 19.3 %collective-permute-start.41 = (f32[128,512]{1,0:T(8,128)}, f32[128,512]{1,0:T(8,128)}, u32[]{:S(2)}, u32[]{:S(2)}) collective-permute-start(f32[128,512]{1,0:T(8,128)} %get-tuple-element.194), channel_id=1, source_target_pairs={{0,2},{1,3},{2,0},{3,1},{4,6},{5,7},{6,4},{7,5},{8,10},{9,11},{10,... | collective-permute-start | bytes 786440 | tf_op jit(solution)/shard_map/ppermute | solution.py:17
  180.3 18.7 %collective-permute-start.42 = (f32[128,512]{1,0:T(8,128)}, f32[128,512]{1,0:T(8,128)}, u32[]{:S(2)}, u32[]{:S(2)}) collective-permute-start(f32[128,512]{1,0:T(8,128)} %get-tuple-element.195), channel_id=1, source_target_pairs={{0,3},{1,2},{2,1},{3,0},{4,7},{5,6},{6,5},{7,4},{8,11},{9,10},{10,... | collective-permute-start | bytes 786440 | tf_op jit(solution)/shard_map/ppermute | solution.py:17
  197.0 13.1 %collective-permute-start.51 = (f32[128,512]{1,0:T(8,128)S(1)}, f32[128,512]{1,0:T(8,128)S(1)}, u32[]{:S(2)}, u32[]{:S(2)}) collective-permute-start(f32[128,512]{1,0:T(8,128)S(1)} %get-tuple-element.208), channel_id=1, source_target_pairs={{0,2},{1,3},{2,0},{3,1},{4,6},{5,7},{6,4},{7,5},{8,10},{9,11},{10,... | collective-permute-start | bytes 786440 | tf_op jit(solution)/shard_map/ppermute | solution.py:17
  197.7 12.5 %collective-permute-start.52 = (f32[128,512]{1,0:T(8,128)S(1)}, f32[128,512]{1,0:T(8,128)S(1)}, u32[]{:S(2)}, u32[]{:S(2)}) collective-permute-start(f32[128,512]{1,0:T(8,128)S(1)} %get-tuple-element.209), channel_id=1, source_target_pairs={{0,3},{1,2},{2,1},{3,0},{4,7},{5,6},{6,5},{7,4},{8,11},{9,10},{10,... | collective-permute-start | bytes 786440 | tf_op jit(solution)/shard_map/ppermute | solution.py:17
  230.9 22.1 %collective-permute-start.55 = (f32[256,512]{1,0:T(8,128)}, f32[256,512]{1,0:T(8,128)}, u32[]{:S(2)}, u32[]{:S(2)}) collective-permute-start(f32[256,512]{1,0:T(8,128)} %copy-done.16), channel_id=1, source_target_pairs={{0,1},{1,0},{2,3},{3,2},{4,5},{5,4},{6,7},{7,6},{8,9},{9,8},{10,11... | collective-permute-start | bytes 1572872 | tf_op jit(solution)/shard_map/ppermute | solution.py:17
  232.1 22.4 %collective-permute-start.54 = (f32[256,512]{1,0:T(8,128)}, f32[256,512]{1,0:T(8,128)}, u32[]{:S(2)}, u32[]{:S(2)}) collective-permute-start(f32[256,512]{1,0:T(8,128)} %copy-done.16), channel_id=1, source_target_pairs={{0,2},{1,3},{2,0},{3,1},{4,6},{5,7},{6,4},{7,5},{8,10},{9,11},{10,... | collective-permute-start | bytes 1572872 | tf_op jit(solution)/shard_map/ppermute | solution.py:17
  232.7 21.8 %collective-permute-start.53 = (f32[256,512]{1,0:T(8,128)}, f32[256,512]{1,0:T(8,128)}, u32[]{:S(2)}, u32[]{:S(2)}) collective-permute-start(f32[256,512]{1,0:T(8,128)} %copy-done.16), channel_id=1, source_target_pairs={{0,3},{1,2},{2,1},{3,0},{4,7},{5,6},{6,5},{7,4},{8,11},{9,10},{10,... | collective-permute-start | bytes 1572872 | tf_op jit(solution)/shard_map/ppermute | solution.py:17
  (61 other events, 473.8 us)

commit v2 on v1

--- a/solution.py
+++ b/solution.py
@@ -120,7 +120,7 @@
             at = pl.multiple_of((place_ref[1] ^ k) * size, size)
             out[...] = multiply(at, size)
     else:
-        size = min(512, width)
+        size = min(1024, width)
         piece = n // len(outs)
         for start in range(0, width, size):
             got = multiply(start, size)

time: 262 us -> 262 us (level)
  no operation moved by 1% of the time
where the time goes in v2:
time: 262 us; the launch traced here: 259 us
  waiting for transfers between devices  93.5 us (36%)
  starting transfers between devices  71.5 us (27%)
  Pallas kernels  61.8 us (24%)
  local copies, waits for them, and re-layouts  20.2 us (8%)
  other arithmetic  7.46 us (3%)
  matrix products  2.9 us (1%)
    ppermute x67, waiting for transfers between devices, swap(): return lax.ppermute(x, axis, [(i, i ^ k) for i in range(n)])  93.5 us
    ppermute x67, starting transfers between devices, swap(): return lax.ppermute(x, axis, [(i, i ^ k) for i in range(n)])  71.5 us
    pallas_call x8, Pallas kernels, product(): pl.pallas_call(functools.partial(product_kernel, spans=spans, dim=dim, bl...  40.6 us
    unnamed x55, local copies, waits for them, and re-layouts  20.1 us
    pallas_call x1, Pallas kernels, inverse_factor(): pl.pallas_call(functools.partial(factor_kernel, scale=scale, size=64, gro...  11.7 us
    pallas_call x1, Pallas kernels, split_array(): pl.pallas_call(split_kernel, out_shape=pltpu.HBM((2, *x.shape), jnp.bfloa...  6.25 us
  transfers between devices with their start and end apart: 67, of which 31 were waited for; matrix products, arithmetic and copies ran while one was open for 2% of the time, Pallas kernels for 22%

profile of v2, /device:TPU:0, one launch (start us, length us, event | category | flops | bytes accessed | tf_op | source)
XLA Modules:
  0.0 258.8 jit_solution(12364115687666633802)
XLA Ops:
  0.6 4.0 %collective-permute-start.2 = (f32[64,2048]{1,0:T(8,128)}, f32[64,2048]{1,0:T(8,128)S(1)}, u32[]{:S(2)}, u32[]{:S(2)}) collective-permute-start(f32[64,2048]{1,0:T(8,128)} %bitcast.6), channel_id=1, source_target_pairs={{0,3},{1,2},{2,1},{3,0},{4,7},{5,6},{6,5},{7,4},{8,11},{9,10},{10,... | collective-permute-start | bytes 1572872 | tf_op jit(solution)/shard_map/ppermute | solution.py:17
  5.2 5.8 %copy-done.3 = f32[2048,2048]{1,0:T(8,128)S(1)} copy-done((f32[2048,2048]{1,0:T(8,128)S(1)}, f32[2048,2048]{1,0:T(8,128)}, u32[]{:S(2)}) %copy-start.3) | copy-done | bytes 16777240
  11.0 6.3 %split_array.1.refs_4_.refs_2_ = bf16[2,2048,2048]{2,1,0:T(8,128)(2,1)} custom-call(f32[2048,2048]{1,0:T(8,128)S(1)} %copy-done.3), custom_call_target="tpu_custom_call" | custom-call | tf_op jit(solution)/shard_map/split_array/pallas_call | solution.py:71
  17.6 10.4 %collective-permute-done.1.refs_2_ = f32[64,2048]{1,0:T(8,128)S(1)} collective-permute-done((f32[64,2048]{1,0:T(8,128)}, f32[64,2048]{1,0:T(8,128)S(1)}, u32[]{:S(2)}, u32[]{:S(2)}) %collective-permute-start.1) | collective-permute-done | bytes 524320 | tf_op jit(solution)/shard_map/ppermute | solution.py:17
  28.3 5.8 %copy-done = bf16[2,2048,2048]{2,1,0:T(8,128)(2,1)S(1)} copy-done((bf16[2,2048,2048]{2,1,0:T(8,128)(2,1)S(1)}, bf16[2,2048,2048]{2,1,0:T(8,128)(2,1)}, u32[]{:S(2)}) %copy-start) | copy-done | bytes 16777240
  34.0 4.1 %product_0.4 = (f32[64,2048]{1,0:T(8,128)S(1)}, f32[64,2048]{1,0:T(8,128)S(1)}) custom-call(s32[2]{0:T(128)S(1)} %get-tuple-element.263.place_ref, f32[64,2048]{1,0:T(8,128)S(1)} %bitcast.9, f32[64,2048]{1,0:T(8,128)S(1)} %collective-permute-done.refs_1_, f32[64,2048]{1,0:T(8,128)S(1)} %collective-permute-done.1.refs_2_, ...), custom_call_target="tpu_custom_call" | custom-call | tf_op jit(solution)/shard_map/product_0/pallas_call | solution.py:137
  48.5 6.7 %collective-permute-done.5 = f32[16,2048]{1,0:T(8,128)S(1)} collective-permute-done((f32[16,2048]{1,0:T(8,128)S(1)}, f32[16,2048]{1,0:T(8,128)S(1)}, u32[]{:S(2)}, u32[]{:S(2)}) %collective-permute-start.5) | collective-permute-done | bytes 131104 | tf_op jit(solution)/shard_map/ppermute | solution.py:17
  59.7 4.1 %product_0.5 = (f32[64,2048]{1,0:T(8,128)S(1)}, f32[64,2048]{1,0:T(8,128)S(1)}) custom-call(s32[2]{0:T(128)S(1)} %get-tuple-element.263.place_ref, f32[64,2048]{1,0:T(8,128)S(1)} %bitcast.10, f32[64,2048]{1,0:T(8,128)S(1)} %collective-permute-done.refs_1_, f32[64,2048]{1,0:T(8,128)S(1)} %collective-permute-done.1.refs_2_, ...), custom_call_target="tpu_custom_call" | custom-call | tf_op jit(solution)/shard_map/product_0/pallas_call | solution.py:137
  63.9 4.1 %collective-permute-done.8 = f32[16,2048]{1,0:T(8,128)S(1)} collective-permute-done((f32[16,2048]{1,0:T(8,128)S(1)}, f32[16,2048]{1,0:T(8,128)S(1)}, u32[]{:S(2)}, u32[]{:S(2)}) %collective-permute-start.8) | collective-permute-done | bytes 131104 | tf_op jit(solution)/shard_map/ppermute | solution.py:17
  72.7 5.6 %product_1.2 = (f32[32,2048]{1,0:T(8,128)S(1)}, f32[32,2048]{1,0:T(8,128)S(1)}, f32[32,2048]{1,0:T(8,128)S(1)}, f32[32,2048]{1,0:T(8,128)S(1)}) custom-call(s32[2]{0:T(128)S(1)} %get-tuple-element.263.place_ref, f32[64,2048]{1,0:T(8,128)S(1)} %constant_dynamic-update-slice_fusion.refs_0_, f32[64,2048]{1,0:T(8,128)S(1)} %collective-permute-done.10.refs_1_, ...), custom_call_target="tpu_custom_call" | custom-call | tf_op jit(solution)/shard_map/product_1/pallas_call | solution.py:137
  87.6 5.5 %collective-permute-done.13 = f32[32,2048]{1,0:T(8,128)S(1)} collective-permute-done((f32[32,2048]{1,0:T(8,128)S(1)}, f32[32,2048]{1,0:T(8,128)S(1)}, u32[]{:S(2)}, u32[]{:S(2)}) %collective-permute-start.13) | collective-permute-done | bytes 262176 | tf_op jit(solution)/shard_map/ppermute | solution.py:17
  96.8 6.5 %collective-permute-done.20.refs_3_ = f32[32,2048]{1,0:T(8,128)S(1)} collective-permute-done((f32[32,2048]{1,0:T(8,128)S(1)}, f32[32,2048]{1,0:T(8,128)S(1)}, u32[]{:S(2)}, u32[]{:S(2)}) %collective-permute-start.20) | collective-permute-done | bytes 262176 | tf_op jit(solution)/shard_map/ppermute | solution.py:17
  106.4 4.3 %product_0.6 = (f32[64,2048]{1,0:T(8,128)S(1)}, f32[64,2048]{1,0:T(8,128)S(1)}) custom-call(s32[2]{0:T(128)S(1)} %get-tuple-element.263.place_ref, f32[32,2048]{1,0:T(8,128)S(1)} %add_subtract_fusion.1.refs_0_, f32[32,2048]{1,0:T(8,128)S(1)} %collective-permute-done.18.refs_1_, f32[32,2048]{1,0:T(8,128)S(1)} %collective-permute-done.19.refs_2_, ...), custom_call_target="tpu_custom_call" | custom-call | tf_op jit(solution)/shard_map/product_0/pallas_call | solution.py:137
  110.8 5.6 %product_1.3 = (f32[32,2048]{1,0:T(8,128)S(1)}, f32[32,2048]{1,0:T(8,128)S(1)}, f32[32,2048]{1,0:T(8,128)S(1)}, f32[32,2048]{1,0:T(8,128)S(1)}) custom-call(s32[2]{0:T(128)S(1)} %get-tuple-element.263.place_ref, f32[64,2048]{1,0:T(8,128)S(1)} %constant_dynamic-update-slice_fusion.4.refs_0_.refs_4_, f32[64,2048]{1,0:T(8,128)S(1)} %collective-permute-done.25.refs_1_.refs_5_, ...), custom_call_target="tpu_custom_call" | custom-call | tf_op jit(solution)/shard_map/product_1/pallas_call | solution.py:137
  126.2 5.1 %collective-permute-done.30 = f32[32,2048]{1,0:T(8,128)S(1)} collective-permute-done((f32[32,2048]{1,0:T(8,128)S(1)}, f32[32,2048]{1,0:T(8,128)S(1)}, u32[]{:S(2)}, u32[]{:S(2)}) %collective-permute-start.30) | collective-permute-done | bytes 262176 | tf_op jit(solution)/shard_map/ppermute | solution.py:17
  137.1 4.5 %collective-permute-done.37.refs_3_ = f32[32,2048]{1,0:T(8,128)S(1)} collective-permute-done((f32[32,2048]{1,0:T(8,128)S(1)}, f32[32,2048]{1,0:T(8,128)S(1)}, u32[]{:S(2)}, u32[]{:S(2)}) %collective-permute-start.37) | collective-permute-done | bytes 262176 | tf_op jit(solution)/shard_map/ppermute | solution.py:17
  145.5 4.1 %product_0.7 = (f32[64,2048]{1,0:T(8,128)S(1)}, f32[64,2048]{1,0:T(8,128)S(1)}) custom-call(s32[2]{0:T(128)S(1)} %get-tuple-element.263.place_ref, f32[32,2048]{1,0:T(8,128)S(1)} %add_subtract_fusion.refs_0_, f32[32,2048]{1,0:T(8,128)S(1)} %collective-permute-done.35.refs_1_, f32[32,2048]{1,0:T(8,128)S(1)} %collective-permute-done.36.refs_2_, ...), custom_call_target="tpu_custom_call" | custom-call | tf_op jit(solution)/shard_map/product_0/pallas_call | solution.py:137
  156.1 6.7 %product_rows.2 = (f32[128,512]{1,0:T(8,128)S(1)}, f32[128,512]{1,0:T(8,128)}, f32[128,512]{1,0:T(8,128)}, f32[128,512]{1,0:T(8,128)}) custom-call(s32[2]{0:T(128)S(1)} %get-tuple-element.264.place_ref, f32[64,2048]{1,0:T(8,128)S(1)} %constant_dynamic-update-slice_fusion.8.refs_0_.refs_2_, f32[64,2048]{1,0:T(8,128)S(1)} %collective-permute-done.38.refs_1_.refs_3_, ...), custom_call_target="tpu_custom_call" | custom-call | tf_op jit(solution)/shard_map/product_rows/pallas_call | solution.py:137
  170.2 3.9 %collective-permute-done.48 = f32[16,2048]{1,0:T(8,128)S(1)} collective-permute-done((f32[16,2048]{1,0:T(8,128)S(1)}, f32[16,2048]{1,0:T(8,128)S(1)}, u32[]{:S(2)}, u32[]{:S(2)}) %collective-permute-start.48) | collective-permute-done | bytes 131104 | tf_op jit(solution)/shard_map/ppermute | solution.py:17
  183.6 5.8 %copy-done.2 = bf16[2,2048,2048]{2,1,0:T(8,128)(2,1)S(1)} copy-done((bf16[2,2048,2048]{2,1,0:T(8,128)(2,1)S(1)}, bf16[2,2048,2048]{2,1,0:T(8,128)(2,1)}, u32[]{:S(2)}) %copy-start.2) | copy-done | bytes 16777240
  189.3 6.1 %product_rows.3 = (f32[128,512]{1,0:T(8,128)S(1)}, f32[128,512]{1,0:T(8,128)S(1)}, f32[128,512]{1,0:T(8,128)S(1)}, f32[128,512]{1,0:T(8,128)S(1)}) custom-call(s32[2]{0:T(128)S(1)} %get-tuple-element.264.place_ref, f32[64,2048]{1,0:T(8,128)S(1)} %constant_dynamic-update-slice_fusion.12.refs_0_.refs_6_, f32[64,2048]{1,0:T(8,128)} %collective-permute-done.49.refs_1_.refs_7_, ...), custom_call_target="tpu_custom_call" | custom-call | tf_op jit(solution)/shard_map/product_rows/pallas_call | solution.py:137
  200.3 4.5 %collective-permute-done.50 = f32[128,512]{1,0:T(8,128)S(1)} collective-permute-done((f32[128,512]{1,0:T(8,128)S(1)}, f32[128,512]{1,0:T(8,128)S(1)}, u32[]{:S(2)}, u32[]{:S(2)}) %collective-permute-start.50) | collective-permute-done | bytes 262176 | tf_op jit(solution)/shard_map/ppermute | solution.py:17
  204.8 5.5 %collective-permute-done.51 = f32[128,512]{1,0:T(8,128)S(1)} collective-permute-done((f32[128,512]{1,0:T(8,128)S(1)}, f32[128,512]{1,0:T(8,128)S(1)}, u32[]{:S(2)}, u32[]{:S(2)}) %collective-permute-start.51) | collective-permute-done | bytes 262176 | tf_op jit(solution)/shard_map/ppermute | solution.py:17
  237.1 11.7 %inverse_factor.1 = f32[256,256]{1,0:T(8,128)S(1)} custom-call(f32[256,256]{1,0:T(8,128)S(1)} %pad_maximum_fusion.gram_ref), custom_call_target="tpu_custom_call" | custom-call | tf_op jit(solution)/shard_map/inverse_factor/pallas_call | solution.py:393
  (208 shorter events, 120.8 us)
Async XLA Ops:
  0.6 17.0 %collective-permute-start.2 = (f32[64,2048]{1,0:T(8,128)}, f32[64,2048]{1,0:T(8,128)S(1)}, u32[]{:S(2)}, u32[]{:S(2)}) collective-permute-start(f32[64,2048]{1,0:T(8,128)} %bitcast.6), channel_id=1, source_target_pairs={{0,3},{1,2},{2,1},{3,0},{4,7},{5,6},{6,5},{7,4},{8,11},{9,10},{10,... | collective-permute-start | bytes 1572872 | tf_op jit(solution)/shard_map/ppermute | solution.py:17
  4.6 23.4 %collective-permute-start.1 = (f32[64,2048]{1,0:T(8,128)}, f32[64,2048]{1,0:T(8,128)S(1)}, u32[]{:S(2)}, u32[]{:S(2)}) collective-permute-start(f32[64,2048]{1,0:T(8,128)} %bitcast.7), channel_id=1, source_target_pairs={{0,2},{1,3},{2,0},{3,1},{4,6},{5,7},{6,4},{7,5},{8,10},{9,11},{10,... | collective-permute-start | bytes 1572872 | tf_op jit(solution)/shard_map/ppermute | solution.py:17
  5.1 23.2 %collective-permute-start = (f32[64,2048]{1,0:T(8,128)}, f32[64,2048]{1,0:T(8,128)S(1)}, u32[]{:S(2)}, u32[]{:S(2)}) collective-permute-start(f32[64,2048]{1,0:T(8,128)} %bitcast.8), channel_id=1, source_target_pairs={{0,1},{1,0},{2,3},{3,2},{4,5},{5,4},{6,7},{7,6},{8,9},{9,8},{10,11... | collective-permute-start | bytes 1572872 | tf_op jit(solution)/shard_map/ppermute | solution.py:17
  68.2 12.3 %collective-permute-start.17 = (f32[16,2048]{1,0:T(8,128)S(1)}, f32[16,2048]{1,0:T(8,128)S(1)}, u32[]{:S(2)}, u32[]{:S(2)}) collective-permute-start(f32[16,2048]{1,0:T(8,128)S(1)} %get-tuple-element.246), channel_id=1, source_target_pairs={{0,24},{4,28},{8,16},{12,20},{16,8},{20,12},{24,0},{28,4},{1,25},{... | collective-permute-start | bytes 393224 | tf_op jit(solution)/shard_map/ppermute | solution.py:17
  79.8 13.2 %collective-permute-start.13 = (f32[32,2048]{1,0:T(8,128)S(1)}, f32[32,2048]{1,0:T(8,128)S(1)}, u32[]{:S(2)}, u32[]{:S(2)}) collective-permute-start(f32[32,2048]{1,0:T(8,128)S(1)} %get-tuple-element.142), channel_id=1, source_target_pairs={{0,2},{1,3},{2,0},{3,1},{4,6},{5,7},{6,4},{7,5},{8,10},{9,11},{10,... | collective-permute-start | bytes 786440 | tf_op jit(solution)/shard_map/ppermute | solution.py:17
  80.6 12.5 %collective-permute-start.14 = (f32[32,2048]{1,0:T(8,128)S(1)}, f32[32,2048]{1,0:T(8,128)S(1)}, u32[]{:S(2)}, u32[]{:S(2)}) collective-permute-start(f32[32,2048]{1,0:T(8,128)S(1)} %get-tuple-element.143), channel_id=1, source_target_pairs={{0,3},{1,2},{2,1},{3,0},{4,7},{5,6},{6,5},{7,4},{8,11},{9,10},{10,... | collective-permute-start | bytes 786440 | tf_op jit(solution)/shard_map/ppermute | solution.py:17
  82.3 12.9 %collective-permute-start.23 = (f32[16,2048]{1,0:T(8,128)S(1)}, f32[16,2048]{1,0:T(8,128)S(1)}, u32[]{:S(2)}, u32[]{:S(2)}) collective-permute-start(f32[16,2048]{1,0:T(8,128)S(1)} %add_add_fusion.2), channel_id=1, source_target_pairs={{0,24},{4,28},{8,16},{12,20},{16,8},{20,12},{24,0},{28,4},{1,25},{... | collective-permute-start | bytes 393224 | tf_op jit(solution)/shard_map/ppermute | solution.py:17
  83.9 12.8 %collective-permute-start.22 = (f32[16,2048]{1,0:T(8,128)S(1)}, f32[16,2048]{1,0:T(8,128)S(1)}, u32[]{:S(2)}, u32[]{:S(2)}) collective-permute-start(f32[16,2048]{1,0:T(8,128)S(1)} %add_add_fusion.2), channel_id=1, source_target_pairs={{0,16},{4,20},{8,24},{12,28},{16,0},{20,4},{24,8},{28,12},{1,17},{... | collective-permute-start | bytes 393224 | tf_op jit(solution)/shard_map/ppermute | solution.py:17
  96.8 14.0 %collective-permute-start.25 = (f32[64,2048]{1,0:T(8,128)S(1)}, f32[64,2048]{1,0:T(8,128)S(1)}, u32[]{:S(2)}, u32[]{:S(2)}) collective-permute-start(f32[64,2048]{1,0:T(8,128)S(1)} %constant_dynamic-update-slice_fusion.4.refs_0_.refs_4_), channel_id=1, source_target_pairs={{0,4},{4,0},{8,12},{12,8},{16,20},{20,16},{24,28},{28,24},{1,5},{5... | collective-permute-start | bytes 1572872 | tf_op jit(solution)/shard_map/ppermute | solution.py:17
  117.3 14.0 %collective-permute-start.30 = (f32[32,2048]{1,0:T(8,128)S(1)}, f32[32,2048]{1,0:T(8,128)S(1)}, u32[]{:S(2)}, u32[]{:S(2)}) collective-permute-start(f32[32,2048]{1,0:T(8,128)S(1)} %get-tuple-element.166), channel_id=1, source_target_pairs={{0,2},{1,3},{2,0},{3,1},{4,6},{5,7},{6,4},{7,5},{8,10},{9,11},{10,... | collective-permute-start | bytes 786440 | tf_op jit(solution)/shard_map/ppermute | solution.py:17
  118.6 12.7 %collective-permute-start.31 = (f32[32,2048]{1,0:T(8,128)S(1)}, f32[32,2048]{1,0:T(8,128)S(1)}, u32[]{:S(2)}, u32[]{:S(2)}) collective-permute-start(f32[32,2048]{1,0:T(8,128)S(1)} %get-tuple-element.167), channel_id=1, source_target_pairs={{0,3},{1,2},{2,1},{3,0},{4,7},{5,6},{6,5},{7,4},{8,11},{9,10},{10,... | collective-permute-start | bytes 786440 | tf_op jit(solution)/shard_map/ppermute | solution.py:17
  120.0 14.1 %collective-permute-start.28 = (f32[16,2048]{1,0:T(8,128)S(1)}, f32[16,2048]{1,0:T(8,128)S(1)}, u32[]{:S(2)}, u32[]{:S(2)}) collective-permute-start(f32[16,2048]{1,0:T(8,128)S(1)} %get-tuple-element.238), channel_id=1, source_target_pairs={{0,24},{4,28},{8,16},{12,20},{16,8},{20,12},{24,0},{28,4},{1,25},{... | collective-permute-start | bytes 393224 | tf_op jit(solution)/shard_map/ppermute | solution.py:17
  122.0 12.9 %collective-permute-start.27 = (f32[16,2048]{1,0:T(8,128)S(1)}, f32[16,2048]{1,0:T(8,128)S(1)}, u32[]{:S(2)}, u32[]{:S(2)}) collective-permute-start(f32[16,2048]{1,0:T(8,128)S(1)} %get-tuple-element.239), channel_id=1, source_target_pairs={{0,16},{4,20},{8,24},{12,28},{16,0},{20,4},{24,8},{28,12},{1,17},{... | collective-permute-start | bytes 393224 | tf_op jit(solution)/shard_map/ppermute | solution.py:17
  132.7 12.7 %collective-permute-start.36 = (f32[32,2048]{1,0:T(8,128)S(1)}, f32[32,2048]{1,0:T(8,128)S(1)}, u32[]{:S(2)}, u32[]{:S(2)}) collective-permute-start(f32[32,2048]{1,0:T(8,128)S(1)} %add_subtract_fusion.refs_0_), channel_id=1, source_target_pairs={{0,2},{1,3},{2,0},{3,1},{4,6},{5,7},{6,4},{7,5},{8,10},{9,11},{10,... | collective-permute-start | bytes 786440 | tf_op jit(solution)/shard_map/ppermute | solution.py:17
  135.0 14.7 %collective-permute-start.34 = (f32[16,2048]{1,0:T(8,128)S(1)}, f32[16,2048]{1,0:T(8,128)S(1)}, u32[]{:S(2)}, u32[]{:S(2)}) collective-permute-start(f32[16,2048]{1,0:T(8,128)S(1)} %add_add_fusion.1), channel_id=1, source_target_pairs={{0,24},{4,28},{8,16},{12,20},{16,8},{20,12},{24,0},{28,4},{1,25},{... | collective-permute-start | bytes 393224 | tf_op jit(solution)/shard_map/ppermute | solution.py:17
  137.0 12.7 %collective-permute-start.33 = (f32[16,2048]{1,0:T(8,128)S(1)}, f32[16,2048]{1,0:T(8,128)S(1)}, u32[]{:S(2)}, u32[]{:S(2)}) collective-permute-start(f32[16,2048]{1,0:T(8,128)S(1)} %add_add_fusion.1), channel_id=1, source_target_pairs={{0,16},{4,20},{8,24},{12,28},{16,0},{20,4},{24,8},{28,12},{1,17},{... | collective-permute-start | bytes 393224 | tf_op jit(solution)/shard_map/ppermute | solution.py:17
  178.1 19.6 %collective-permute-start.40 = (f32[128,512]{1,0:T(8,128)}, f32[128,512]{1,0:T(8,128)}, u32[]{:S(2)}, u32[]{:S(2)}) collective-permute-start(f32[128,512]{1,0:T(8,128)} %get-tuple-element.193), channel_id=1, source_target_pairs={{0,1},{1,0},{2,3},{3,2},{4,5},{5,4},{6,7},{7,6},{8,9},{9,8},{10,11... | collective-permute-start | bytes 786440 | tf_op jit(solution)/shard_map/ppermute | solution.py:17
  179.7 19.3 %collective-permute-start.41 = (f32[128,512]{1,0:T(8,128)}, f32[128,512]{1,0:T(8,128)}, u32[]{:S(2)}, u32[]{:S(2)}) collective-permute-start(f32[128,512]{1,0:T(8,128)} %get-tuple-element.194), channel_id=1, source_target_pairs={{0,2},{1,3},{2,0},{3,1},{4,6},{5,7},{6,4},{7,5},{8,10},{9,11},{10,... | collective-permute-start | bytes 786440 | tf_op jit(solution)/shard_map/ppermute | solution.py:17
  180.3 18.7 %collective-permute-start.42 = (f32[128,512]{1,0:T(8,128)}, f32[128,512]{1,0:T(8,128)}, u32[]{:S(2)}, u32[]{:S(2)}) collective-permute-start(f32[128,512]{1,0:T(8,128)} %get-tuple-element.195), channel_id=1, source_target_pairs={{0,3},{1,2},{2,1},{3,0},{4,7},{5,6},{6,5},{7,4},{8,11},{9,10},{10,... | collective-permute-start | bytes 786440 | tf_op jit(solution)/shard_map/ppermute | solution.py:17
  197.1 13.1 %collective-permute-start.51 = (f32[128,512]{1,0:T(8,128)S(1)}, f32[128,512]{1,0:T(8,128)S(1)}, u32[]{:S(2)}, u32[]{:S(2)}) collective-permute-start(f32[128,512]{1,0:T(8,128)S(1)} %get-tuple-element.208), channel_id=1, source_target_pairs={{0,2},{1,3},{2,0},{3,1},{4,6},{5,7},{6,4},{7,5},{8,10},{9,11},{10,... | collective-permute-start | bytes 786440 | tf_op jit(solution)/shard_map/ppermute | solution.py:17
  197.7 12.5 %collective-permute-start.52 = (f32[128,512]{1,0:T(8,128)S(1)}, f32[128,512]{1,0:T(8,128)S(1)}, u32[]{:S(2)}, u32[]{:S(2)}) collective-permute-start(f32[128,512]{1,0:T(8,128)S(1)} %get-tuple-element.209), channel_id=1, source_target_pairs={{0,3},{1,2},{2,1},{3,0},{4,7},{5,6},{6,5},{7,4},{8,11},{9,10},{10,... | collective-permute-start | bytes 786440 | tf_op jit(solution)/shard_map/ppermute | solution.py:17
  230.9 22.1 %collective-permute-start.55 = (f32[256,512]{1,0:T(8,128)}, f32[256,512]{1,0:T(8,128)}, u32[]{:S(2)}, u32[]{:S(2)}) collective-permute-start(f32[256,512]{1,0:T(8,128)} %copy-done.16), channel_id=1, source_target_pairs={{0,1},{1,0},{2,3},{3,2},{4,5},{5,4},{6,7},{7,6},{8,9},{9,8},{10,11... | collective-permute-start | bytes 1572872 | tf_op jit(solution)/shard_map/ppermute | solution.py:17
  232.1 22.5 %collective-permute-start.54 = (f32[256,512]{1,0:T(8,128)}, f32[256,512]{1,0:T(8,128)}, u32[]{:S(2)}, u32[]{:S(2)}) collective-permute-start(f32[256,512]{1,0:T(8,128)} %copy-done.16), channel_id=1, source_target_pairs={{0,2},{1,3},{2,0},{3,1},{4,6},{5,7},{6,4},{7,5},{8,10},{9,11},{10,... | collective-permute-start | bytes 1572872 | tf_op jit(solution)/shard_map/ppermute | solution.py:17
  232.8 21.8 %collective-permute-start.53 = (f32[256,512]{1,0:T(8,128)}, f32[256,512]{1,0:T(8,128)}, u32[]{:S(2)}, u32[]{:S(2)}) collective-permute-start(f32[256,512]{1,0:T(8,128)} %copy-done.16), channel_id=1, source_target_pairs={{0,3},{1,2},{2,1},{3,0},{4,7},{5,6},{6,5},{7,4},{8,11},{9,10},{10,... | collective-permute-start | bytes 1572872 | tf_op jit(solution)/shard_map/ppermute | solution.py:17
  (61 other events, 473.8 us)
